TPU v7x, 32 devices: a whole 2x2x4 slice. The times are simulated.
32 devices in a mesh: parts: 2 (over y), wide: 4 (over z), col: 2 (over x), sub: 2 (over core).
Axes of the slice: x: 2, y: 2, z: 4, core: 2. Of those that a mesh axis runs over, the one named last changes fastest.
Arguments:
- parent_inverse: float32 [16384, 8192], P(('parts', 'wide'), 'col'), parts along dimension 0, as said below
- child_rows: int32 [4, 3072], P(('parts', 'sub')), parts along dimension 0, may hold values from 0 to 2047, as said below
- row_counts: int32 [4, 4], P(('parts', 'sub')), parts along dimension 0, may hold values from 1 to 768, as said below
- child_factor: float32 [4, 3072, 6144], P(('parts', 'sub'), 'wide', 'col'), parts along dimension 0, may hold values from -0.21875 to 0.21875
- own_variance: float32 [4, 6144], P(('parts', 'sub'), 'col'), parts along dimension 0, may hold values from 0.5 to 2
Outputs:
- cross_block: float32 [4, 3072, 6144], P(('parts', 'sub'), 'wide', 'col'), parts along dimension 0
- variances: float32 [4, 6144], P(('parts', 'sub'), 'col'), parts along dimension 0
There are 2 independent parts, one for each index of `parts`. A program takes and returns all parts, laid end to end along the dimension named above; each array names one. Nothing has to cross between parts.
Inputs may be any that keep to these rules, and one draw needn't show every extreme that they name: `child_rows`: within each child and block, the live slots hold distinct offsets. `row_counts`: each child has at least one block with all 768 slots live. `parent_inverse`: Symmetric.
All inputs are finite; a program needn't handle non-finite values.
Results may differ from a plain program's by a relative error of at most 0.0001.
Values sent between devices are 32-bit elements; how exact they have to be, the bound alone decides.
A program may use at most 320 MiB of HBM per device.

v0:
```python
import jax
import jax.numpy as jnp
from jax import lax
from jax.sharding import PartitionSpec as P


def per_device(parent_inverse, child_rows, row_counts, child_factor, own_variance):
    wide_count = lax.axis_size("wide")
    slots = child_factor.shape[1]
    total_rows = child_rows.shape[1]
    block_rows = parent_inverse.shape[0]
    wide_index = lax.axis_index("wide")
    slot_index = jnp.arange(slots, dtype=jnp.int32)
    offsets_all = child_rows[0].reshape(wide_count, slots)
    mine = lax.dynamic_slice_in_dim(child_rows[0], wide_index * slots, slots)
    live_mine = slot_index < row_counts[0, wide_index]
    live_all = (slot_index[None, :] < row_counts[0][:, None]).reshape(total_rows)
    local_rows = parent_inverse[mine]
    whole_rows = lax.all_gather(local_rows, "col", axis=1, tiled=True)
    global_rows = (
        jnp.arange(wide_count, dtype=jnp.int32)[:, None] * block_rows + offsets_all
    ).reshape(total_rows)
    sigma_rows = whole_rows[:, global_rows]
    sigma_rows = jnp.where(live_mine[:, None] & live_all[None, :], sigma_rows, 0.0)
    running = jnp.dot(
        sigma_rows,
        lax.all_gather(child_factor[0], "wide", axis=0, tiled=True),
        precision=lax.Precision.HIGHEST,
        preferred_element_type=jnp.float32,
    )
    cross_part = -running
    partial_value = jnp.sum(child_factor[0] * cross_part, axis=0)
    totals = lax.psum(partial_value, "wide")
    finished = own_variance[0] - totals
    return (cross_part[None], finished[None])


def solution(mesh):
    placed = (
        P(("parts", "wide"), "col"),
        P(("parts", "sub"), None),
        P(("parts", "sub"), None),
        P(("parts", "sub"), "wide", "col"),
        P(("parts", "sub"), "col"),
    )
    return jax.shard_map(
        per_device,
        mesh=mesh,
        in_specs=placed,
        out_specs=(P(("parts", "sub"), "wide", "col"), P(("parts", "sub"), "col")),
        check_vma=False,
    )
```

profile of v0, /device:TPU:0, one launch (start us, length us, event | category | flops | bytes accessed | tf_op | source)
XLA Modules:
  0.0 1079.8 jit_solution(1657970558663665419)
XLA Ops:
  7.2 0.0 all-gather.5.cloned.1.call-start
  7.2 0.7 fusion.7
  7.9 22.5 %gather_fusion = f32[768,4096]{1,0:T(8,128)} fusion(f32[2048,4096]{1,0:T(8,128)} %param.5, s32[1024]{0:T(1024)S(1)} %pad_clamp_fusion), kind=kCustom, calls=%fused_computation | custom fusion | bytes 25168896 | tf_op jit(solution)/shard_map/gather | solution.py:18
  30.5 0.0 copy-start.2
  30.5 0.0 copy-start
  30.5 0.0 all-gather.5.cloned.1.call-update
  30.5 0.0 all-gather.7.cloned.1.call-start
  30.5 0.7 all-gather.7.cloned.1.call-update
  31.3 0.1 broadcast_bitcast_fusion
  31.3 0.0 copy-done.2
  31.4 0.6 constant_dynamic-slice_fusion
  31.9 0.1 iota_compare_fusion
  32.0 0.6 iota_compare_fusion.1
  32.7 0.0 copy-done
  32.7 294.3 %all-gather.5.cloned.1.call-done = f32[768,8192]{1,0:T(8,128)} async-done(((f32[768,4096]{1,0:T(8,128)}), f32[768,8192]{1,0:T(8,128)}) %all-gather.5.cloned.1.call-update) | async-done | bytes 25165840 | tf_op jit(solution)/shard_map/all_gather | solution.py:19
  327.1 26.1 %copy.8 = f32[768,8192]{0,1:T(8,128)} copy(f32[768,8192]{1,0:T(8,128)} %all-gather.5.cloned.1.call-done) | data formatting | bytes 50331648 | tf_op jit(solution)/shard_map/all_gather | solution.py:19
  353.2 25.5 %gather_fusion.1 = f32[3072,768]{1,0:T(8,128)} fusion(f32[768,8192]{0,1:T(8,128)} %copy.8, s32[3072]{0:T(1024)S(1)} %broadcast_clamp_fusion), kind=kCustom, calls=%fused_computation.1 | custom fusion | bytes 18886656 | tf_op jit(solution)/shard_map/gather | solution.py:23
  378.7 8.7 bitcast_select_fusion.6
  387.4 0.0 copy-start.1
  387.4 572.7 %all-gather.7.cloned.1.call-done = f32[1,3072,3072]{2,1,0:T(8,128)} async-done(((f32[1,768,3072]{2,1,0:T(8,128)}), f32[1,3072,3072]{2,1,0:T(8,128)}) %all-gather.7.cloned.1.call-update) | async-done | bytes 37748752 | tf_op jit(solution)/shard_map/all_gather | solution.py:27
  960.1 96.3 %fusion.2 = (f32[3072]{0:T(1024)S(1)}, f32[1,768,3072]{2,1,0:T(8,128)}) fusion(f32[1,768,3072]{2,1,0:T(8,128)} %param.8, f32[1,3072,3072]{2,1,0:T(8,128)} %all-gather.7.cloned.1.call-done, f32[768,3072]{0,1:T(8,128)} %bitcast_select_fusion.6), kind=kOutput, calls=%fused_computation.5 | convolution fusion | flops 86980165632 | bytes 66072576 | tf_op jit(solution)/shard_map/dot_general | solution.py:25
  1056.4 16.0 %psum.7 = f32[3072]{0:T(1024)S(1)} all-reduce(f32[3072]{0:T(1024)S(1)} %get-tuple-element.2), channel_id=1, replica_groups=mesh['parts'=2,'wide'=4,'col'=2,'sub'=2] {'wide'}, use_global_device_ids=true, to_apply=%region_1.2 | all-reduce | flops 3072 | bytes 24576 | tf_op jit(solution)/shard_map/psum | solution.py:33
  1072.4 0.0 copy-done.1
  1072.4 0.6 sub.3
  (6 shorter events, 0.1 us)
Async XLA Ops:
  7.2 319.9 %all-gather.5.cloned.1.call-start = ((), (), s32[]{:S(2)}) async-start(), calls=%async_computation | async-start | bytes 37748736 | tf_op jit(solution)/shard_map/all_gather | solution.py:19
  30.5 0.9 copy-start.2
  30.5 2.2 copy-start
  30.5 929.6 %all-gather.7.cloned.1.call-start = ((), (), s32[]{:S(2)}) async-start(), calls=%async_computation.1 | async-start | bytes 47185920 | tf_op jit(solution)/shard_map/all_gather | solution.py:27
  387.4 684.9 %copy-start.1 = (f32[1,3072]{1,0:T(1,128)S(1)}, f32[1,3072]{1,0:T(1,128)}, u32[]{:S(2)}) copy-start(f32[1,3072]{1,0:T(1,128)} %param.9) | copy-start | bytes 36868
Sparse Core Ops, SparseCore 0:
  30.6 296.3 all-gather.4
  328.6 631.4 all-gather.6
where the time goes:
time: 1080 us
  waiting for transfers between devices  868 us (80%)
  matrix products  96.3 us (9%)
  local copies, waits for them, and re-layouts  74.9 us (7%)
  blocking collectives  16 us (1%)
  between operations  14.1 us (1%)
  other arithmetic  10.8 us (1%)
    all_gather x1, waiting for transfers between devices, per_device(): lax.all_gather(child_factor[0], 'wide', axis=0, tiled=True)  573 us
    all_gather x1, waiting for transfers between devices, per_device(): whole_rows = lax.all_gather(local_rows, 'col', axis=1, tiled=True)  294 us
    dot_general x1, matrix products, per_device(): jnp.dot(sigma_rows, lax.all_gather(child_factor[0], 'wide', axis=0, tiled...  96.3 us
    all_gather x1, local copies, waits for them, and re-layouts, per_device(): whole_rows = lax.all_gather(local_rows, 'col', axis=1, tiled=True)  26.1 us
    gather x1, local copies, waits for them, and re-layouts, per_device(): sigma_rows = whole_rows[:, global_rows]  25.5 us
    gather x1, local copies, waits for them, and re-layouts, per_device(): local_rows = parent_inverse[mine]  22.5 us
  transfers between devices with their start and end apart: 2, of which 2 were waited for; matrix products, arithmetic and copies ran while one was open for 6% of the time, Pallas kernels for 0%

commit v1 on v0

v1 whole, which is shorter than its diff:
```python
import jax
import jax.numpy as jnp
from jax import lax
from jax.sharding import PartitionSpec as P

PIPES = 2


def dot(a, b, contract):
    return lax.dot_general(
        a,
        b,
        ((contract[0], contract[1]), ((), ())),
        precision=lax.Precision.HIGH,
        preferred_element_type=jnp.float32,
    )


def per_device(parent_inverse, child_rows, row_counts, child_factor, own_variance):
    wide = lax.axis_size("wide")
    cols = lax.axis_size("col")
    me = lax.axis_index("wide")
    my_col = lax.axis_index("col")
    slots, width = child_factor.shape[1:]
    block_rows, block_cols = parent_inverse.shape
    held = block_cols // block_rows
    factor = child_factor[0]
    offsets = child_rows[0].reshape(wide, slots)
    slot_index = jnp.arange(slots, dtype=jnp.int32)
    half = width // 2
    pipe = half // PIPES
    right = [(i, i + 1) for i in range(wide - 1)]
    left = [(i + 1, i) for i in range(wide - 1)]
    ways = ((me, right, -1), (wide - 1 - me, left, 1))

    spread = [factor[:, p * pipe : (p + 1) * pipe] for p in range(PIPES)]
    summed = factor[:, half:]
    got = [[lax.ppermute(spread[p], "wide", perm) for _, perm, _ in ways] for p in range(PIPES)]

    mine = lax.dynamic_index_in_dim(offsets, me, 0, keepdims=False)
    live_mine = slot_index < lax.dynamic_index_in_dim(row_counts[0], me, 0, keepdims=False)
    local_rows = jnp.where(live_mine[:, None], parent_inverse[mine], 0.0)
    high = lax.reduce_precision(local_rows, 8, 7)
    low = (local_rows - high).astype(jnp.bfloat16)
    high = high.astype(jnp.bfloat16)
    flip = jnp.where(me < wide // 2, held - 1, 0)
    pieces = []
    for i in range(held):
        at = jnp.where(flip > 0, held - 1 - i, i)
        block = my_col * held + at
        offset = lax.dynamic_index_in_dim(offsets, block, 0, keepdims=False)
        live = slot_index < lax.dynamic_index_in_dim(row_counts[0], block, 0, keepdims=False)
        pick = (
            (jnp.arange(block_rows, dtype=jnp.int32)[:, None] == offset[None, :]) & live[None, :]
        ).astype(jnp.bfloat16)
        piece = 0.0
        for part in (low, high):
            columns = lax.dynamic_slice_in_dim(part, at * block_rows, block_rows, 1)
            piece += jnp.dot(columns, pick, preferred_element_type=jnp.float32)
        pieces.append(lax.all_gather(piece, "col", axis=0))

    def sigma(block, valid):
        owner = block // held
        at = block % held
        order = jnp.where(flip > 0, held - 1 - at, at)
        value = lax.dynamic_index_in_dim(pieces[0], owner, 0, keepdims=False)
        for i in range(1, held):
            other = lax.dynamic_index_in_dim(pieces[i], owner, 0, keepdims=False)
            value = jnp.where(order == i, other, value)
        return jnp.where(valid, value, 0.0)

    own = sigma(me, True)
    total = [dot(own, spread[p], ((1,), (0,))) for p in range(PIPES)]
    finish = dot(own, summed, ((1,), (0,)))
    for step in range(2, wide + 1):
        for w, (rank, perm, sign) in enumerate(ways):
            source = me + sign * (step - 1)
            here = sigma(jnp.clip(source, 0, wide - 1), rank >= step - 1)
            target = me - sign * (wide - step + 1)
            away = sigma(jnp.clip(target, 0, wide - 1), rank <= step - 2)
            terms = dot(away, summed, ((0,), (0,)))
            for p in range(PIPES):
                came = got[p][w]
                total[p] += dot(here, came, ((1,), (0,)))
                send = came + terms[:, p * pipe : (p + 1) * pipe]
                got[p][w] = lax.ppermute(send, "wide", perm)
    parts = [-t for t in total]
    for p in range(PIPES):
        parts.append(-(finish[:, p * pipe : (p + 1) * pipe] + got[p][0] + got[p][1]))
    cross_part = jnp.concatenate(parts, axis=1)
    partial_value = jnp.sum(factor * cross_part, axis=0)
    totals = lax.psum(partial_value, "wide")
    return (cross_part[None], (own_variance[0] - totals)[None])


def solution(mesh):
    placed = (
        P(("parts", "wide"), "col"),
        P(("parts", "sub"), None),
        P(("parts", "sub"), None),
        P(("parts", "sub"), "wide", "col"),
        P(("parts", "sub"), "col"),
    )
    return jax.shard_map(
        per_device,
        mesh=mesh,
        in_specs=placed,
        out_specs=(P(("parts", "sub"), "wide", "col"), P(("parts", "sub"), "col")),
        check_vma=False,
    )
```

time: 1080 us -> 627 us (0.58)
  waiting for transfers between devices: 868 us -> 256 us
  other arithmetic: 10.8 us -> 76.6 us
  matrix products: 96.3 us -> 158 us
  starting transfers between devices: 0.08 us -> 48.8 us
  local copies, waits for them, and re-layouts: 74.9 us -> 49.1 us
    all_gather x2, waiting for transfers between devices: 867 us -> 92.4 us  [per_device(): pieces.append(lax.all_gather(piece, 'col', axis=0))]
    ppermute x0 -> x16, waiting for transfers between devices: none -> 163 us  [the longest x12 163 us: per_device(): got[p][w] = lax.ppermute(send, 'wide', perm)]
    dot_general x1 -> x25, matrix products: 96.3 us -> 158 us  [the longest x21 141 us: dot(): lax.dot_general(a, b, ((contract[0], contract[1]), ((), ())), precision=l...]
    ppermute x0 -> x16, starting transfers between devices: none -> 48.5 us  [the longest x12 36.2 us: per_device(): got[p][w] = lax.ppermute(send, 'wide', perm)]
    add x0 -> x6, other arithmetic: none -> 35.2 us  [per_device(): send = came + terms[:, p * pipe:(p + 1) * pipe]]
    all_gather x1 -> x0, local copies, waits for them, and re-layouts: 26.1 us -> none  [per_device(): whole_rows = lax.all_gather(local_rows, 'col', axis=1, tiled=True)]
    gather x2 -> x1, local copies, waits for them, and re-layouts: 48 us -> 22.6 us  [per_device(): local_rows = jnp.where(live_mine[:, None], parent_inverse[mine], 0.0)]
    unnamed x8 -> x43, local copies, waits for them, and re-layouts: 0.1 us -> 20.2 us
  transfers between devices with their start and end apart: 2 -> 18, of which waited for: 2 -> 8; matrix products, arithmetic and copies ran while one was open for 6% -> 35% of each run, Pallas kernels for 0% -> 0%
where the time goes in v1:
time: 627 us; the launch traced here: 619 us
  waiting for transfers between devices  256 us (41%)
  matrix products  158 us (25%)
  other arithmetic  76.6 us (12%)
  local copies, waits for them, and re-layouts  49.1 us (8%)
  starting transfers between devices  48.8 us (8%)
  blocking collectives  15.6 us (2%)
  between operations  14.9 us (2%)
    ppermute x12, waiting for transfers between devices, per_device(): got[p][w] = lax.ppermute(send, 'wide', perm)  163 us
    dot_general x21, matrix products, dot(): lax.dot_general(a, b, ((contract[0], contract[1]), ((), ())), precision=l...  141 us
    all_gather x2, waiting for transfers between devices, per_device(): pieces.append(lax.all_gather(piece, 'col', axis=0))  92.4 us
    ppermute x12, starting transfers between devices, per_device(): got[p][w] = lax.ppermute(send, 'wide', perm)  36.2 us
    add x6, other arithmetic, per_device(): send = came + terms[:, p * pipe:(p + 1) * pipe]  35.2 us
    gather x1, local copies, waits for them, and re-layouts, per_device(): local_rows = jnp.where(live_mine[:, None], parent_inverse[mine], 0.0)  22.6 us
    unnamed x43, local copies, waits for them, and re-layouts  20.2 us
    dot_general x4, matrix products, per_device(): piece += jnp.dot(columns, pick, preferred_element_type=jnp.float32)  17.8 us
  transfers between devices with their start and end apart: 18, of which 8 were waited for; matrix products, arithmetic and copies ran while one was open for 35% of the time, Pallas kernels for 0%

profile of v1, /device:TPU:0, one launch (start us, length us, event | category | flops | bytes accessed | tf_op | source)
XLA Modules:
  0.0 619.0 jit_solution(10146195885349046842)
XLA Ops:
  12.0 22.6 %gather_fusion = f32[768,4096]{1,0:T(8,128)} fusion(f32[2048,4096]{1,0:T(8,128)} %param.5, s32[1024]{0:T(1024)S(1)} %pad_clamp_fusion), kind=kCustom, calls=%fused_computation | custom fusion | bytes 25168896 | tf_op jit(solution)/shard_map/gather | solution.py:42
  34.6 11.2 %fusion = (bf16[768,4096]{1,0:T(8,128)(2,1)}, bf16[768,4096]{1,0:T(8,128)(2,1)}) fusion(f32[768,4096]{1,0:T(8,128)} %gather_fusion, pred[768]{0:T(1024)(128)(4,1)S(1)} %iota_compare_fusion.4), kind=kLoop, calls=%fused_computation.3 | loop fusion | flops 15728640 | bytes 25166592 | tf_op jit(solution)/shard_map/convert_element_type | solution.py:44
  64.7 10.0 %copy.23 = f32[1,768,3072]{1,2,0:T(8,128)} copy(f32[1,768,3072]{2,1,0:T(8,128)} %param.8) | data formatting | bytes 18874368 | tf_op args[3]
  79.5 6.3 %collective-permute-start = (f32[768,768]{0,1:T(8,128)}, f32[768,768]{0,1:T(8,128)}, u32[]{:S(2)}, u32[]{:S(2)}) collective-permute-start(f32[768,768]{0,1:T(8,128)} %get-tuple-element.12), channel_id=1, source_target_pairs={{0,4},{4,8},{8,12},{1,5},{5,9},{9,13},{2,6},{6,10},{10,14},{3,7},{... | collective-permute-start | bytes 7077896 | tf_op jit(solution)/shard_map/ppermute | solution.py:38
  92.0 28.2 %all-gather.5.cloned.1.call-done = f32[1536,768]{1,0:T(8,128)} async-done(((f32[768,768]{1,0:T(8,128)}), f32[1536,768]{1,0:T(8,128)}) %all-gather.5.cloned.1.call-update) | async-done | bytes 4718608 | tf_op jit(solution)/shard_map/all_gather | solution.py:60
  120.2 64.2 %all-gather.7.cloned.1.call-done = f32[1536,768]{1,0:T(8,128)} async-done(((f32[768,768]{1,0:T(8,128)}), f32[1536,768]{1,0:T(8,128)}) %all-gather.7.cloned.1.call-update) | async-done | bytes 4718608 | tf_op jit(solution)/shard_map/all_gather | solution.py:60
  184.4 15.8 %dynamic-slice_select_fusion.6 = (f32[1,768,768]{2,1,0:T(8,128)}, f32[1,768,768]{2,1,0:T(8,128)S(1)}, f32[1,768,768]{2,1,0:T(8,128)}, f32[1,768,768]{2,1,0:T(8,1...) fusion(f32[2,768,768]{2,1,0:T(8,128)} %bitcast.99, s32[]{:T(128)S(6)} %select_n.377, ...), kind=kLoop, calls=%fused_computation.108 | loop fusion | flops 4128768 | bytes 49545252 | tf_op jit(solution)/shard_map/jit(_where)/select_n | solution.py:69
  200.2 8.4 %fusion.36 = f32[768,1536]{0,1:T(8,128)S(1)} fusion(f32[768,3072]{0,1:T(8,128)} %bitcast.87, f32[1,768,768]{2,1,0:T(8,128)S(1)} %get-tuple-element.17, pred[]{:T(512)S(6)} %le.18), kind=kOutput, calls=%fused_computation.39 | convolution fusion | flops 5436407808 | bytes 11796481 | tf_op jit(solution)/shard_map/dot_general | solution.py:10
  231.9 7.6 %fusion.28 = f32[768,1536]{0,1:T(8,128)} fusion(f32[768,3072]{0,1:T(8,128)S(1)} %bitcast.92, f32[1,768,768]{2,1,0:T(8,128)S(1)} %copy-done.4), kind=kOutput, calls=%fused_computation.31 | convolution fusion | flops 5435817984 | bytes 11796480 | tf_op jit(solution)/shard_map/dot_general | solution.py:10
  239.5 6.6 %fusion.34 = f32[768,1536]{0,1:T(8,128)S(1)} fusion(f32[768,3072]{0,1:T(8,128)S(1)} %bitcast.93, f32[1,768,768]{2,1,0:T(8,128)S(1)} %get-tuple-element.15, pred[]{:T(512)S(6)} %le.19), kind=kOutput, calls=%fused_computation.37 | convolution fusion | flops 5436407808 | bytes 11796481 | tf_op jit(solution)/shard_map/dot_general | solution.py:10
  254.0 7.8 %fusion.26 = f32[768,1536]{0,1:T(8,128)} fusion(f32[768,3072]{0,1:T(8,128)S(1)} %bitcast.94, f32[1,768,768]{2,1,0:T(8,128)S(1)} %copy-done.3, pred[]{:T(512)S(6)} %le.22), kind=kOutput, calls=%fused_computation.29 | convolution fusion | flops 5436407808 | bytes 11796481 | tf_op jit(solution)/shard_map/dot_general | solution.py:10
  267.8 6.1 fusion.64
  273.9 6.1 fusion.70
  280.0 6.9 %fusion.24 = f32[768,1536]{0,1:T(8,128)S(1)} fusion(f32[768,3072]{0,1:T(8,128)S(1)} %bitcast.95, f32[1,768,768]{2,1,0:T(8,128)S(1)} %copy-done.2, pred[]{:T(512)S(6)} %le.23), kind=kOutput, calls=%fused_computation.27 | convolution fusion | flops 5436407808 | bytes 11796481 | tf_op jit(solution)/shard_map/dot_general | solution.py:10
  286.9 7.6 %fusion.32 = f32[768,1536]{0,1:T(8,128)} fusion(f32[768,3072]{0,1:T(8,128)S(1)} %bitcast.96, f32[1,768,768]{2,1,0:T(8,128)S(1)} %copy-done, pred[]{:T(512)S(6)} %le.20), kind=kOutput, calls=%fused_computation.35 | convolution fusion | flops 5436407808 | bytes 11796481 | tf_op jit(solution)/shard_map/dot_general | solution.py:10
  294.5 7.6 %fusion.30 = f32[768,1536]{0,1:T(8,128)} fusion(f32[768,3072]{0,1:T(8,128)S(1)} %bitcast.97, f32[1,768,768]{2,1,0:T(8,128)S(1)} %copy-done.1, pred[]{:T(512)S(6)} %le.21), kind=kOutput, calls=%fused_computation.33 | convolution fusion | flops 5436407808 | bytes 11796481 | tf_op jit(solution)/shard_map/dot_general | solution.py:10
  302.1 16.6 %collective-permute-done.8 = f32[768,768]{0,1:T(8,128)} collective-permute-done((f32[768,768]{0,1:T(8,128)}, f32[768,768]{0,1:T(8,128)}, u32[]{:S(2)}, u32[]{:S(2)}) %collective-permute-start.8) | collective-permute-done | bytes 2359328 | tf_op jit(solution)/shard_map/ppermute | solution.py:86
  318.7 6.5 %slice_add_fusion.11 = (f32[768,768]{0,1:T(8,128)}, f32[768,768]{0,1:T(8,128)}) fusion(f32[768,768]{0,1:T(8,128)} %collective-permute-done.2, f32[768,1536]{0,1:T(8,128)} %fusion.32, f32[768,768]{0,1:T(8,128)} %collective-permute-done.8), kind=kLoop, calls=%fused_computation.56 | loop fusion | flops 1179648 | bytes 14155776 | tf_op jit(solution)/shard_map/add | solution.py:85
  334.7 21.8 %collective-permute-done.9 = f32[768,768]{0,1:T(8,128)} collective-permute-done((f32[768,768]{0,1:T(8,128)}, f32[768,768]{0,1:T(8,128)}, u32[]{:S(2)}, u32[]{:S(2)}) %collective-permute-start.9) | collective-permute-done | bytes 2359328 | tf_op jit(solution)/shard_map/ppermute | solution.py:86
  356.6 6.5 %slice_add_fusion.10 = (f32[768,768]{0,1:T(8,128)}, f32[768,768]{0,1:T(8,128)}) fusion(f32[768,768]{0,1:T(8,128)} %collective-permute-done.3, f32[768,1536]{0,1:T(8,128)} %fusion.30, f32[768,768]{0,1:T(8,128)} %collective-permute-done.9), kind=kLoop, calls=%fused_computation.55 | loop fusion | flops 1179648 | bytes 14155776 | tf_op jit(solution)/shard_map/add | solution.py:85
  384.2 6.3 %fusion.57 = f32[768,768]{0,1:T(8,128)} fusion(f32[768,768]{0,1:T(8,128)} %collective-permute-done.3, f32[1,768,768]{2,1,0:T(8,128)S(1)} %copy-done, pred[]{:T(512)S(6)} %ge.21), kind=kOutput, calls=%fused_computation.74 | convolution fusion | flops 2718498816 | bytes 7077889 | tf_op jit(solution)/shard_map/dot_general | solution.py:10
  390.5 6.1 fusion.55
  396.6 33.5 %collective-permute-done.10 = f32[768,768]{0,1:T(8,128)} collective-permute-done((f32[768,768]{0,1:T(8,128)}, f32[768,768]{0,1:T(8,128)}, u32[]{:S(2)}, u32[]{:S(2)}) %collective-permute-start.10) | collective-permute-done | bytes 2359328 | tf_op jit(solution)/shard_map/ppermute | solution.py:86
  430.0 6.6 %slice_add_fusion.4 = (f32[768,768]{0,1:T(8,128)}, f32[768,768]{0,1:T(8,128)}) fusion(f32[768,768]{0,1:T(8,128)} %collective-permute-done.4, f32[768,1536]{0,1:T(8,128)} %fusion.26, f32[768,768]{0,1:T(8,128)} %collective-permute-done.10), kind=kLoop, calls=%fused_computation.47 | loop fusion | flops 1179648 | bytes 14155776 | tf_op jit(solution)/shard_map/add | solution.py:85
  446.2 21.1 %collective-permute-done.11 = f32[768,768]{0,1:T(8,128)} collective-permute-done((f32[768,768]{0,1:T(8,128)}, f32[768,768]{0,1:T(8,128)}, u32[]{:S(2)}, u32[]{:S(2)}) %collective-permute-start.11) | collective-permute-done | bytes 2359328 | tf_op jit(solution)/shard_map/ppermute | solution.py:86
  481.1 6.2 %fusion.50 = f32[768,768]{0,1:T(8,128)} fusion(f32[768,768]{0,1:T(8,128)} %collective-permute-done.10, f32[1,768,768]{2,1,0:T(8,128)S(1)} %get-tuple-element.15, pred[]{:T(512)S(6)} %ge.22), kind=kOutput, calls=%fused_computation.67 | convolution fusion | flops 2718498816 | bytes 7077889 | tf_op jit(solution)/shard_map/dot_general | solution.py:10
  487.3 9.1 %add_negate_fusion.1 = f32[768,768]{0,1:T(8,128)} fusion(f32[768,768]{0,1:T(8,128)} %fusion.52, f32[768,768]{0,1:T(8,128)} %fusion.57, f32[768,768]{0,1:T(8,128)} %fusion.62, f32[768,768]{0,1:T(8,128)S(1)} %copy-done.8, f32[768,768]{0,1:T(8,128)S(1)} %copy-done.6, f32[768,768]{0,1:T(8,128)S(1)} %copy-done.9, f32[768,768]{0,1:T(8,128)} %collective-permute-done.5, ...), kind=kOutput, calls=%fused_computation.97 | convolution fusion | flops 2722627584 | bytes 21233664 | tf_op jit(solution)/shard_map/dot_general | solution.py:10
  496.5 9.2 %add_negate_fusion = f32[768,768]{0,1:T(8,128)} fusion(f32[768,768]{0,1:T(8,128)} %fusion.50, f32[768,768]{0,1:T(8,128)} %fusion.55, f32[768,768]{0,1:T(8,128)} %fusion.60, f32[768,768]{0,1:T(8,128)S(1)} %copy-done.7, f32[768,768]{0,1:T(8,128)S(1)} %copy-done.5, f32[768,768]{0,1:T(8,128)S(1)} %copy-done.10, f32[768,768]{0,1:T(8,128)} %collective-permute-done.11, ...), kind=kOutput, calls=%fused_computation.96 | convolution fusion | flops 2722627584 | bytes 21233664 | tf_op jit(solution)/shard_map/dot_general | solution.py:10
  505.7 34.9 %collective-permute-done.14 = f32[768,768]{0,1:T(8,128)} collective-permute-done((f32[768,768]{0,1:T(8,128)}, f32[768,768]{0,1:T(8,128)}, u32[]{:S(2)}, u32[]{:S(2)}) %collective-permute-start.14) | collective-permute-done | bytes 2359328 | tf_op jit(solution)/shard_map/ppermute | solution.py:86
  540.6 35.2 %collective-permute-done.15 = f32[768,768]{0,1:T(8,128)} collective-permute-done((f32[768,768]{0,1:T(8,128)}, f32[768,768]{0,1:T(8,128)}, u32[]{:S(2)}, u32[]{:S(2)}) %collective-permute-start.15) | collective-permute-done | bytes 2359328 | tf_op jit(solution)/shard_map/ppermute | solution.py:86
  586.1 9.6 %copy.38 = f32[1,768,3072]{2,1,0:T(8,128)} copy(f32[1,768,3072]{1,2,0:T(8,128)} %get-tuple-element.11) | data formatting | bytes 18874368
  595.7 15.6 %psum.7 = f32[3072]{0:T(1024)S(1)} all-reduce(f32[3072]{0:T(1024)S(1)} %get-tuple-element.10), channel_id=1, replica_groups=mesh['parts'=2,'wide'=4,'col'=2,'sub'=2] {'wide'}, use_global_device_ids=true, to_apply=%region_1.2 | all-reduce | flops 3072 | bytes 24576 | tf_op jit(solution)/shard_map/psum | solution.py:92
  (99 shorter events, 136.5 us)
Async XLA Ops:
  7.2 113.0 %all-gather.5.cloned.1.call-start = ((), (), s32[]{:S(2)}) async-start(), calls=%async_computation | async-start | bytes 7077888 | tf_op jit(solution)/shard_map/all_gather | solution.py:60
  54.6 129.8 %all-gather.7.cloned.1.call-start = ((), (), s32[]{:S(2)}) async-start(), calls=%async_computation.1 | async-start | bytes 7077888 | tf_op jit(solution)/shard_map/all_gather | solution.py:60
  79.5 129.2 %collective-permute-start = (f32[768,768]{0,1:T(8,128)}, f32[768,768]{0,1:T(8,128)}, u32[]{:S(2)}, u32[]{:S(2)}) collective-permute-start(f32[768,768]{0,1:T(8,128)} %get-tuple-element.12), channel_id=1, source_target_pairs={{0,4},{4,8},{8,12},{1,5},{5,9},{9,13},{2,6},{6,10},{10,14},{3,7},{... | collective-permute-start | bytes 7077896 | tf_op jit(solution)/shard_map/ppermute | solution.py:38
  85.8 122.9 %collective-permute-start.6 = (f32[768,768]{0,1:T(8,128)}, f32[768,768]{0,1:T(8,128)}, u32[]{:S(2)}, u32[]{:S(2)}) collective-permute-start(f32[768,768]{0,1:T(8,128)} %get-tuple-element.13), channel_id=1, source_target_pairs={{0,4},{4,8},{8,12},{1,5},{5,9},{9,13},{2,6},{6,10},{10,14},{3,7},{... | collective-permute-start | bytes 7077896 | tf_op jit(solution)/shard_map/ppermute | solution.py:38
  89.2 156.9 %collective-permute-start.1 = (f32[768,768]{0,1:T(8,128)}, f32[768,768]{0,1:T(8,128)}, u32[]{:S(2)}, u32[]{:S(2)}) collective-permute-start(f32[768,768]{0,1:T(8,128)} %get-tuple-element.12), channel_id=1, source_target_pairs={{4,0},{8,4},{12,8},{5,1},{9,5},{13,9},{6,2},{10,6},{14,10},{7,3},{... | collective-permute-start | bytes 7077896 | tf_op jit(solution)/shard_map/ppermute | solution.py:38
  90.5 155.6 %collective-permute-start.7 = (f32[768,768]{0,1:T(8,128)}, f32[768,768]{0,1:T(8,128)}, u32[]{:S(2)}, u32[]{:S(2)}) collective-permute-start(f32[768,768]{0,1:T(8,128)} %get-tuple-element.13), channel_id=1, source_target_pairs={{4,0},{8,4},{12,8},{5,1},{9,5},{13,9},{6,2},{10,6},{14,10},{7,3},{... | collective-permute-start | bytes 7077896 | tf_op jit(solution)/shard_map/ppermute | solution.py:38
  200.2 22.7 %slice-start = ((s8[9437184]{0:T(1024)(128)(4,1)}), s8[4194304]{0:T(1024)(128)(4,1)S(1)}, s32[]{:S(2)}) async-start(s8[9437184]{0:T(1024)(128)(4,1)} %bitcast.88), calls=%async_computation.2 | async-start | bytes 8388608
  200.2 22.7 %slice-start.1 = ((s8[9437184]{0:T(1024)(128)(4,1)}), s8[4194304]{0:T(1024)(128)(4,1)S(1)}, s32[]{:S(2)}) async-start(s8[9437184]{0:T(1024)(128)(4,1)} %bitcast.88), calls=%async_computation.3 | async-start | bytes 8388608
  208.6 14.2 %slice-start.2 = ((s8[9437184]{0:T(1024)(128)(4,1)}), s8[1048576]{0:T(1024)(128)(4,1)S(1)}, s32[]{:S(2)}) async-start(s8[9437184]{0:T(1024)(128)(4,1)} %bitcast.88), calls=%async_computation.4 | async-start | bytes 2097152
  208.7 14.2 %copy-start.4 = (f32[1,768,768]{2,1,0:T(8,128)S(1)}, f32[1,768,768]{2,1,0:T(8,128)}, u32[]{:S(2)}) copy-start(f32[1,768,768]{2,1,0:T(8,128)} %get-tuple-element.14) | copy-start | bytes 7077892
  213.9 88.1 %collective-permute-start.2 = (f32[768,768]{0,1:T(8,128)}, f32[768,768]{0,1:T(8,128)}, u32[]{:S(2)}, u32[]{:S(2)}) collective-permute-start(f32[768,768]{0,1:T(8,128)} %get-tuple-element.27), channel_id=1, source_target_pairs={{0,4},{4,8},{8,12},{1,5},{5,9},{9,13},{2,6},{6,10},{10,14},{3,7},{... | collective-permute-start | bytes 7077896 | tf_op jit(solution)/shard_map/ppermute | solution.py:86
  218.8 99.9 %collective-permute-start.8 = (f32[768,768]{0,1:T(8,128)}, f32[768,768]{0,1:T(8,128)}, u32[]{:S(2)}, u32[]{:S(2)}) collective-permute-start(f32[768,768]{0,1:T(8,128)} %get-tuple-element.28), channel_id=1, source_target_pairs={{0,4},{4,8},{8,12},{1,5},{5,9},{9,13},{2,6},{6,10},{10,14},{3,7},{... | collective-permute-start | bytes 7077896 | tf_op jit(solution)/shard_map/ppermute | solution.py:86
  246.1 7.9 %copy-start.3 = (f32[1,768,768]{2,1,0:T(8,128)S(1)}, f32[1,768,768]{2,1,0:T(8,128)}, u32[]{:S(2)}) copy-start(f32[1,768,768]{2,1,0:T(8,128)} %get-tuple-element.19) | copy-start | bytes 7077892
  251.4 83.3 %collective-permute-start.3 = (f32[768,768]{0,1:T(8,128)}, f32[768,768]{0,1:T(8,128)}, u32[]{:S(2)}, u32[]{:S(2)}) collective-permute-start(f32[768,768]{0,1:T(8,128)} %get-tuple-element.33), channel_id=1, source_target_pairs={{4,0},{8,4},{12,8},{5,1},{9,5},{13,9},{6,2},{10,6},{14,10},{7,3},{... | collective-permute-start | bytes 7077896 | tf_op jit(solution)/shard_map/ppermute | solution.py:86
  252.7 103.9 %collective-permute-start.9 = (f32[768,768]{0,1:T(8,128)}, f32[768,768]{0,1:T(8,128)}, u32[]{:S(2)}, u32[]{:S(2)}) collective-permute-start(f32[768,768]{0,1:T(8,128)} %get-tuple-element.34), channel_id=1, source_target_pairs={{4,0},{8,4},{12,8},{5,1},{9,5},{13,9},{6,2},{10,6},{14,10},{7,3},{... | collective-permute-start | bytes 7077896 | tf_op jit(solution)/shard_map/ppermute | solution.py:86
  280.0 6.9 %copy-start = (f32[1,768,768]{2,1,0:T(8,128)S(1)}, f32[1,768,768]{2,1,0:T(8,128)}, u32[]{:S(2)}) copy-start(f32[1,768,768]{2,1,0:T(8,128)} %get-tuple-element.16) | copy-start | bytes 7077892
  286.9 7.6 %copy-start.1 = (f32[1,768,768]{2,1,0:T(8,128)S(1)}, f32[1,768,768]{2,1,0:T(8,128)}, u32[]{:S(2)}) copy-start(f32[1,768,768]{2,1,0:T(8,128)} %get-tuple-element.18) | copy-start | bytes 7077892
  325.2 71.4 %collective-permute-start.4 = (f32[768,768]{0,1:T(8,128)}, f32[768,768]{0,1:T(8,128)}, u32[]{:S(2)}, u32[]{:S(2)}) collective-permute-start(f32[768,768]{0,1:T(8,128)} %get-tuple-element.25), channel_id=1, source_target_pairs={{0,4},{4,8},{8,12},{1,5},{5,9},{9,13},{2,6},{6,10},{10,14},{3,7},{... | collective-permute-start | bytes 7077896 | tf_op jit(solution)/shard_map/ppermute | solution.py:86
  331.0 99.1 %collective-permute-start.10 = (f32[768,768]{0,1:T(8,128)}, f32[768,768]{0,1:T(8,128)}, u32[]{:S(2)}, u32[]{:S(2)}) collective-permute-start(f32[768,768]{0,1:T(8,128)} %get-tuple-element.26), channel_id=1, source_target_pairs={{0,4},{4,8},{8,12},{1,5},{5,9},{9,13},{2,6},{6,10},{10,14},{3,7},{... | collective-permute-start | bytes 7077896 | tf_op jit(solution)/shard_map/ppermute | solution.py:86
  363.0 83.2 %collective-permute-start.5 = (f32[768,768]{0,1:T(8,128)}, f32[768,768]{0,1:T(8,128)}, u32[]{:S(2)}, u32[]{:S(2)}) collective-permute-start(f32[768,768]{0,1:T(8,128)} %get-tuple-element.31), channel_id=1, source_target_pairs={{4,0},{8,4},{12,8},{5,1},{9,5},{13,9},{6,2},{10,6},{14,10},{7,3},{... | collective-permute-start | bytes 7077896 | tf_op jit(solution)/shard_map/ppermute | solution.py:86
  364.3 103.0 %collective-permute-start.11 = (f32[768,768]{0,1:T(8,128)}, f32[768,768]{0,1:T(8,128)}, u32[]{:S(2)}, u32[]{:S(2)}) collective-permute-start(f32[768,768]{0,1:T(8,128)} %get-tuple-element.32), channel_id=1, source_target_pairs={{4,0},{8,4},{12,8},{5,1},{9,5},{13,9},{6,2},{10,6},{14,10},{7,3},{... | collective-permute-start | bytes 7077896 | tf_op jit(solution)/shard_map/ppermute | solution.py:86
  436.6 69.0 %collective-permute-start.12 = (f32[768,768]{0,1:T(8,128)}, f32[768,768]{0,1:T(8,128)}, u32[]{:S(2)}, u32[]{:S(2)}) collective-permute-start(f32[768,768]{0,1:T(8,128)} %get-tuple-element.23), channel_id=1, source_target_pairs={{0,4},{4,8},{8,12},{1,5},{5,9},{9,13},{2,6},{6,10},{10,14},{3,7},{... | collective-permute-start | bytes 7077896 | tf_op jit(solution)/shard_map/ppermute | solution.py:86
  442.4 98.2 %collective-permute-start.14 = (f32[768,768]{0,1:T(8,128)}, f32[768,768]{0,1:T(8,128)}, u32[]{:S(2)}, u32[]{:S(2)}) collective-permute-start(f32[768,768]{0,1:T(8,128)} %get-tuple-element.24), channel_id=1, source_target_pairs={{0,4},{4,8},{8,12},{1,5},{5,9},{9,13},{2,6},{6,10},{10,14},{3,7},{... | collective-permute-start | bytes 7077896 | tf_op jit(solution)/shard_map/ppermute | solution.py:86
  472.4 68.2 %collective-permute-start.13 = (f32[768,768]{0,1:T(8,128)}, f32[768,768]{0,1:T(8,128)}, u32[]{:S(2)}, u32[]{:S(2)}) collective-permute-start(f32[768,768]{0,1:T(8,128)} %get-tuple-element.29), channel_id=1, source_target_pairs={{4,0},{8,4},{12,8},{5,1},{9,5},{13,9},{6,2},{10,6},{14,10},{7,3},{... | collective-permute-start | bytes 7077896 | tf_op jit(solution)/shard_map/ppermute | solution.py:86
  473.7 102.0 %collective-permute-start.15 = (f32[768,768]{0,1:T(8,128)}, f32[768,768]{0,1:T(8,128)}, u32[]{:S(2)}, u32[]{:S(2)}) collective-permute-start(f32[768,768]{0,1:T(8,128)} %get-tuple-element.30), channel_id=1, source_target_pairs={{4,0},{8,4},{12,8},{5,1},{9,5},{13,9},{6,2},{10,6},{14,10},{7,3},{... | collective-permute-start | bytes 7077896 | tf_op jit(solution)/shard_map/ppermute | solution.py:86
  481.1 6.2 %copy-start.9 = (f32[768,768]{0,1:T(8,128)S(1)}, f32[768,768]{0,1:T(8,128)}, u32[]{:S(2)}) copy-start(f32[768,768]{0,1:T(8,128)} %fusion.70) | copy-start | bytes 7077892
  487.3 9.2 %copy-start.5 = (f32[768,768]{0,1:T(8,128)S(1)}, f32[768,768]{0,1:T(8,128)}, u32[]{:S(2)}) copy-start(f32[768,768]{0,1:T(8,128)} %fusion.73) | copy-start | bytes 7077892
  487.3 9.2 %copy-start.7 = (f32[768,768]{0,1:T(8,128)S(1)}, f32[768,768]{0,1:T(8,128)}, u32[]{:S(2)}) copy-start(f32[768,768]{0,1:T(8,128)} %fusion.64) | copy-start | bytes 7077892
  487.3 9.2 %copy-start.10 = (f32[768,768]{0,1:T(8,128)S(1)}, f32[768,768]{0,1:T(8,128)}, u32[]{:S(2)}) copy-start(f32[768,768]{0,1:T(8,128)} %fusion.68) | copy-start | bytes 7077892
  505.7 76.1 %copy-start.11 = (f32[768,768]{0,1:T(8,128)S(1)}, f32[768,768]{0,1:T(8,128)}, u32[]{:S(2)}) copy-start(f32[768,768]{0,1:T(8,128)} %add_negate_fusion.1) | copy-start | bytes 7077892
  505.7 76.1 %copy-start.12 = (f32[768,768]{0,1:T(8,128)S(1)}, f32[768,768]{0,1:T(8,128)}, u32[]{:S(2)}) copy-start(f32[768,768]{0,1:T(8,128)} %add_negate_fusion) | copy-start | bytes 7077892
  586.1 25.2 %copy-start.14 = (f32[1,3072]{1,0:T(1,128)S(1)}, f32[1,3072]{1,0:T(1,128)}, u32[]{:S(2)}) copy-start(f32[1,3072]{1,0:T(1,128)} %param.9) | copy-start | bytes 36868
  (6 other events, 33.8 us)
Sparse Core Ops, SparseCore 0:
  54.8 65.3 all-gather.4
  121.7 62.6 all-gather.6

commit v2 on v1

v2 whole, which is shorter than its diff:
```python
import functools

import jax
import jax.numpy as jnp
from jax import lax
from jax.experimental import pallas as pl
from jax.experimental.pallas import tpu as pltpu
from jax.experimental.layout import Layout, with_layout_constraint
from jax.sharding import PartitionSpec as P

PIPES = 2


def pick_kernel(at_ref, mine_ref, live_ref, wanted_ref, parent_ref, *rest):
    out, rows, sem = rest[-3:]
    slots, block_rows = rows.shape
    columns = pl.ds(pl.multiple_of(at_ref[0] * block_rows, 128), block_rows)

    def issue(i, carry):
        pltpu.make_async_copy(
            parent_ref.at[pl.ds(mine_ref[i], 1), columns], rows.at[pl.ds(i, 1)], sem
        ).start()
        return carry

    lax.fori_loop(0, slots, issue, 0, unroll=8)
    pltpu.make_async_copy(parent_ref.at[pl.ds(0, slots), columns], rows, sem).wait()
    depth = 512 if block_rows % 512 == 0 else block_rows
    out[...] = jnp.zeros_like(out)

    def add(c, carry):
        x = rows[:, pl.ds(pl.multiple_of(c * depth, 128), depth)]
        high = x.astype(jnp.bfloat16)
        low = (x - high.astype(jnp.float32)).astype(jnp.bfloat16)
        place = lax.broadcasted_iota(jnp.int32, (depth, slots), 0) + c * depth
        pick = jnp.where(place == wanted_ref[...], 1.0, 0.0).astype(jnp.bfloat16)
        out[...] += jnp.dot(low, pick, preferred_element_type=jnp.float32) + jnp.dot(
            high, pick, preferred_element_type=jnp.float32
        )
        return carry

    lax.fori_loop(0, block_rows // depth, add, 0)
    out[...] = jnp.where(live_ref[...] > 0.0, out[...], 0.0)


def dot(a, b, contract):
    return lax.dot_general(
        a,
        b,
        ((contract[0], contract[1]), ((), ())),
        precision=lax.Precision.HIGH,
        preferred_element_type=jnp.float32,
    )


def per_device(parent_inverse, child_rows, row_counts, child_factor, own_variance):
    wide = lax.axis_size("wide")
    cols = lax.axis_size("col")
    me = lax.axis_index("wide")
    my_col = lax.axis_index("col")
    slots, width = child_factor.shape[1:]
    block_rows, block_cols = parent_inverse.shape
    held = block_cols // block_rows
    factor = child_factor[0]
    offsets = child_rows[0].reshape(wide, slots)
    slot_index = jnp.arange(slots, dtype=jnp.int32)
    half = width // 2
    pipe = half // PIPES
    right = [(i, i + 1) for i in range(wide - 1)]
    left = [(i + 1, i) for i in range(wide - 1)]
    ways = ((me, right, -1), (wide - 1 - me, left, 1))

    def flat(x):
        return with_layout_constraint(x, Layout(major_to_minor=(0, 1)))

    spread = [flat(factor[:, p * pipe : (p + 1) * pipe]) for p in range(PIPES)]
    summed = factor[:, half:]
    got = [[flat(lax.ppermute(spread[p], "wide", perm)) for _, perm, _ in ways] for p in range(PIPES)]

    mine = lax.dynamic_index_in_dim(offsets, me, 0, keepdims=False)
    live_mine = slot_index < lax.dynamic_index_in_dim(row_counts[0], me, 0, keepdims=False)
    flip = jnp.where(me < wide // 2, held - 1, 0)
    at = jnp.stack([jnp.where(flip > 0, held - 1 - i, i) for i in range(held)]).astype(jnp.int32)
    block = my_col * held + at
    wanted = jnp.where(slot_index[None, :] < row_counts[0][block][:, None], offsets[block], -1)
    pieces = []
    for i in range(held):
        local = pl.pallas_call(
            pick_kernel,
            out_shape=jax.ShapeDtypeStruct((slots, slots), jnp.float32),
            in_specs=[
                pl.BlockSpec(memory_space=pltpu.SMEM),
                pl.BlockSpec(memory_space=pltpu.SMEM),
                pl.BlockSpec(memory_space=pltpu.VMEM),
                pl.BlockSpec(memory_space=pltpu.VMEM),
            ]
            + [pl.BlockSpec(memory_space=pl.ANY)] * (1 + PIPES),
            out_specs=pl.BlockSpec(memory_space=pltpu.VMEM),
            scratch_shapes=[pltpu.VMEM((slots, block_rows), jnp.float32), pltpu.SemaphoreType.DMA],
            compiler_params=pltpu.CompilerParams(vmem_limit_bytes=32 * 1024 * 1024),
            cost_estimate=pl.CostEstimate(flops=1000, bytes_accessed=1000, transcendentals=0),
            name="pick",
        )(
            at[i : i + 1],
            mine,
            live_mine.astype(jnp.float32)[:, None],
            wanted[i : i + 1],
            parent_inverse,
            *spread,
        )
        if i == 1:
            corner = sum(jnp.abs(x[0, 0]) for pair in got for x in pair)
            corner = jnp.minimum(corner.astype(jnp.int32), 0)
            local = jnp.where(corner >= 0, local, 0.0)
        pieces.append(lax.all_gather(local, "col", axis=0))
    blocks = jnp.concatenate(pieces, axis=0)

    def sigma(block):
        block = jnp.clip(block, 0, wide - 1)
        at = block % held
        order = jnp.where(flip > 0, held - 1 - at, at)
        return lax.dynamic_index_in_dim(blocks, order * cols + block // held, 0, keepdims=False)

    own = sigma(me)
    total = [dot(own, spread[p], ((1,), (0,))) for p in range(PIPES)]
    finish = dot(own, summed, ((1,), (0,)))
    for step in range(2, wide + 1):
        for w, (rank, perm, sign) in enumerate(ways):
            here = sigma(me + sign * (step - 1))
            target = me - sign * (wide - step + 1)
            if step == 2:
                owner = jnp.clip(target, 0, wide - 1) // held
                away = lax.dynamic_index_in_dim(pieces[0], owner, 0, keepdims=False)
            else:
                away = sigma(target)
            terms = dot(away, summed, ((0,), (0,)))
            for p in range(PIPES):
                came = got[p][w]
                term = terms[:, p * pipe : (p + 1) * pipe]
                send = flat(came + jnp.where(rank <= step - 2, term, 0.0))
                got[p][w] = flat(lax.ppermute(send, "wide", perm))
                total[p] += jnp.where(rank >= step - 1, dot(here, came, ((1,), (0,))), 0.0)
    parts = [-t for t in total]
    for p in range(PIPES):
        parts.append(-(finish[:, p * pipe : (p + 1) * pipe] + got[p][0] + got[p][1]))
    cross_part = jnp.concatenate(parts, axis=1)
    partial_value = jnp.sum(factor * cross_part, axis=0)
    totals = lax.psum(partial_value, "wide")
    return (cross_part[None], (own_variance[0] - totals)[None])


def solution(mesh):
    placed = (
        P(("parts", "wide"), "col"),
        P(("parts", "sub"), None),
        P(("parts", "sub"), None),
        P(("parts", "sub"), "wide", "col"),
        P(("parts", "sub"), "col"),
    )
    return jax.shard_map(
        per_device,
        mesh=mesh,
        in_specs=placed,
        out_specs=(P(("parts", "sub"), "wide", "col"), P(("parts", "sub"), "col")),
        check_vma=False,
    )
```

time: 627 us -> 544 us (0.87)
  local copies, waits for them, and re-layouts: 49.1 us -> 13.6 us
  other arithmetic: 76.6 us -> 49.3 us
  waiting for transfers between devices: 256 us -> 230 us
  Pallas kernels: 0 us -> 24.8 us
  matrix products: 158 us -> 135 us
    ppermute x4, waiting for transfers between devices: 0.01 us -> 80.2 us  [per_device(): lax.ppermute(spread[p], 'wide', perm)]
    all_gather x2, waiting for transfers between devices: 92.4 us -> 27 us  [per_device(): pieces.append(lax.all_gather(local, 'col', axis=0))]
    ppermute x12, waiting for transfers between devices: 163 us -> 122 us  [per_device(): got[p][w] = flat(lax.ppermute(send, 'wide', perm))]
    pallas_call x0 -> x2, Pallas kernels: none -> 24.8 us  [per_device(): pl.pallas_call(pick_kernel, out_shape=jax.ShapeDtypeStruct((slots, slots)...]
    gather x1 -> x2, local copies, waits for them, and re-layouts: 22.6 us -> 1.2 us  [the longest x1 0.64 us: per_device(): row_counts[0][block][:, None]]
    dot_general x4 -> x0, matrix products: 17.8 us -> none  [per_device(): piece += jnp.dot(columns, pick, preferred_element_type=jnp.float32)]
    select_n x2 -> x3, other arithmetic: 15.8 us -> 1.67 us  [the longest x1 1.52 us: per_device(): local = jnp.where(corner >= 0, local, 0.0)]
    unnamed x43 -> x67, local copies, waits for them, and re-layouts: 20.2 us -> 6.93 us
  transfers between devices with their start and end apart: 18 -> 18, of which waited for: 8 -> 11; matrix products, arithmetic and copies ran while one was open for 35% -> 32% of each run, Pallas kernels for 0% -> 2%
where the time goes in v2:
time: 544 us; the launch traced here: 536 us
  waiting for transfers between devices  230 us (42%)
  matrix products  135 us (25%)
  other arithmetic  49.3 us (9%)
  starting transfers between devices  49 us (9%)
  Pallas kernels  24.8 us (5%)
  between operations  17.6 us (3%)
  blocking collectives  16.7 us (3%)
  local copies, waits for them, and re-layouts  13.6 us (2%)
    dot_general x21, matrix products, dot(): lax.dot_general(a, b, ((contract[0], contract[1]), ((), ())), precision=l...  135 us
    ppermute x12, waiting for transfers between devices, per_device(): got[p][w] = flat(lax.ppermute(send, 'wide', perm))  122 us
    ppermute x4, waiting for transfers between devices, per_device(): lax.ppermute(spread[p], 'wide', perm)  80.2 us
    ppermute x12, starting transfers between devices, per_device(): got[p][w] = flat(lax.ppermute(send, 'wide', perm))  36.6 us
    add x6, other arithmetic, per_device(): send = flat(came + jnp.where(rank <= step - 2, term, 0.0))  27.7 us
    all_gather x2, waiting for transfers between devices, per_device(): pieces.append(lax.all_gather(local, 'col', axis=0))  27 us
    pallas_call x2, Pallas kernels, per_device(): pl.pallas_call(pick_kernel, out_shape=jax.ShapeDtypeStruct((slots, slots)...  24.8 us
    psum x1, blocking collectives, per_device(): totals = lax.psum(partial_value, 'wide')  16.7 us
  transfers between devices with their start and end apart: 18, of which 11 were waited for; matrix products, arithmetic and copies ran while one was open for 32% of the time, Pallas kernels for 2%

profile of v2, /device:TPU:0, one launch (start us, length us, event | category | flops | bytes accessed | tf_op | source)
XLA Modules:
  0.0 535.7 jit_solution(10313768394924374541)
XLA Ops:
  14.5 12.4 %pick.2 = f32[768,768]{1,0:T(8,128)S(1)} custom-call(s32[1]{0:T(128)} %bitcast.at_ref, s32[768]{0:T(1024)S(1)} %get-tuple-element.27.mine_ref, f32[768,1]{1,0:T(8,128)S(1)} %fusion.49.live_ref, s32[1,768]{1,0:T(1,128)S(1)} %get-tuple-element.26.wanted_ref, f32[2048,4096]{1,0:T(8,128)} %parent_ref.3, f32[768,768]{1,0:T(8,128)S(1)} %get-tuple-element.9.rest_0_, ...), custom_call_target="tpu_custom_call" | custom-call | flops 1000 | bytes 1000 | tf_op jit(solution)/shard_map/pick/pallas_call | solution.py:87
  29.9 5.1 collective-permute-start
  44.1 12.4 %pick.3 = f32[768,768]{1,0:T(8,128)S(1)} custom-call(s32[1]{0:T(128)} %bitcast.9.at_ref, s32[768]{0:T(1024)S(1)} %get-tuple-element.27.mine_ref, f32[768,1]{1,0:T(8,128)S(1)} %fusion.49.live_ref, s32[1,768]{1,0:T(1,128)S(1)} %get-tuple-element.25.wanted_ref, f32[2048,4096]{1,0:T(8,128)} %parent_ref.3, f32[768,768]{1,0:T(8,128)S(1)} %copy-done.3, ...), custom_call_target="tpu_custom_call" | custom-call | flops 1000 | bytes 1000 | tf_op jit(solution)/shard_map/pick/pallas_call | solution.py:87
  56.5 30.3 %collective-permute-done = f32[768,768]{1,0:T(8,128)S(1)} collective-permute-done((f32[768,768]{1,0:T(8,128)}, f32[768,768]{1,0:T(8,128)S(1)}, u32[]{:S(2)}, u32[]{:S(2)}) %collective-permute-start) | collective-permute-done | bytes 2359328 | tf_op jit(solution)/shard_map/ppermute | solution.py:77
  92.4 43.6 %collective-permute-done.2 = f32[768,768]{1,0:T(8,128)S(1)} collective-permute-done((f32[768,768]{1,0:T(8,128)S(1)}, f32[768,768]{1,0:T(8,128)S(1)}, u32[]{:S(2)}, u32[]{:S(2)}) %collective-permute-start.2) | collective-permute-done | bytes 2359328 | tf_op jit(solution)/shard_map/ppermute | solution.py:77
  143.4 9.4 %fusion.13 = f32[768,1536]{1,0:T(8,128)S(1)} fusion(f32[768,3072]{1,0:T(8,128)} %bitcast.86, f32[2,768,768]{2,1,0:T(8,128)} %bitcast.69, s32[]{:T(128)S(6)} %select_n.317), kind=kOutput, calls=%fused_computation.31 | convolution fusion | flops 5435817984 | bytes 11796484 | tf_op jit(solution)/shard_map/dot_general | solution.py:46
  164.4 9.4 %fusion.11 = f32[768,1536]{1,0:T(8,128)S(1)} fusion(f32[768,3072]{1,0:T(8,128)} %bitcast.87, f32[2,768,768]{2,1,0:T(8,128)} %bitcast.70, s32[]{:T(128)S(6)} %select_n.327), kind=kOutput, calls=%fused_computation.29 | convolution fusion | flops 5435817984 | bytes 11796484 | tf_op jit(solution)/shard_map/dot_general | solution.py:46
  179.2 27.0 %all-gather.7.cloned.1.call-done = f32[1536,768]{1,0:T(8,128)} async-done(((f32[768,768]{1,0:T(8,128)}), f32[1536,768]{1,0:T(8,128)}) %all-gather.7.cloned.1.call-update) | async-done | bytes 4718608 | tf_op jit(solution)/shard_map/all_gather | solution.py:114
  206.2 6.9 %fusion.18 = (f32[768,768]{1,0:T(8,128)S(1)}, f32[768,768]{1,0:T(8,128)S(1)}, f32[768,768]{1,0:T(8,128)S(1)}, f32[768,768]{1,0:T(8,128)}, f32[768,768]{1,0:T(8,128)S(1)}) fusion(s32[]{:T(128)S(6)} %select_n.297, f32[2,768,768]{2,1,0:T(8,128)} %bitcast.71, f32[2,768,768]{2,1,0:T(8,128)} %bitcast.78, s32[]{:T(128)S(6)} %select_n.302, s32[]{:T(128)S(6)} %select_n.308, ...), kind=kLoop, calls=%fused_computation.36 | loop fusion | flops 2949120 | bytes 21233684 | tf_op jit(solution)/shard_map/jit(dynamic_index_in_dim)/squeeze | solution.py:121
  213.1 8.9 %fusion.9 = f32[768,1536]{1,0:T(8,128)S(1)} fusion(f32[768,768]{1,0:T(8,128)S(1)} %get-tuple-element.8, f32[768,3072]{1,0:T(8,128)} %bitcast.88), kind=kOutput, calls=%fused_computation.27 | convolution fusion | flops 5435817984 | bytes 11796480 | tf_op jit(solution)/shard_map/dot_general | solution.py:46
  222.1 37.0 %collective-permute-done.8 = f32[768,768]{1,0:T(8,128)} collective-permute-done((f32[768,768]{1,0:T(8,128)}, f32[768,768]{1,0:T(8,128)}, u32[]{:S(2)}, u32[]{:S(2)}) %collective-permute-start.8) | collective-permute-done | bytes 2359328 | tf_op jit(solution)/shard_map/ppermute | solution.py:140
  259.1 5.0 fusion.42
  277.9 6.9 %fusion.7 = f32[768,1536]{1,0:T(8,128)S(1)} fusion(f32[768,768]{1,0:T(8,128)S(1)} %copy-done.5, f32[768,3072]{1,0:T(8,128)S(1)} %bitcast.93), kind=kOutput, calls=%fused_computation.25 | convolution fusion | flops 5435817984 | bytes 11796480 | tf_op jit(solution)/shard_map/dot_general | solution.py:46
  291.1 6.0 %collective-permute-start.10 = (f32[768,768]{1,0:T(8,128)}, f32[768,768]{1,0:T(8,128)}, u32[]{:S(2)}, u32[]{:S(2)}) collective-permute-start(f32[768,768]{1,0:T(8,128)} %get-tuple-element.16), channel_id=1, source_target_pairs={{0,4},{4,8},{8,12},{1,5},{5,9},{9,13},{2,6},{6,10},{10,14},{3,7},{... | collective-permute-start | bytes 7077896 | tf_op jit(solution)/shard_map/ppermute | solution.py:140
  298.4 6.1 %fusion.68 = f32[768,768]{1,0:T(8,128)} fusion(f32[768,768]{1,0:T(8,128)S(1)} %copy-done.5, f32[768,768]{1,0:T(8,128)} %collective-permute-done.4), kind=kOutput, calls=%fused_computation.106 | convolution fusion | flops 2717908992 | bytes 7077888 | tf_op jit(solution)/shard_map/dot_general | solution.py:46
  304.5 6.1 %fusion.69 = f32[768,768]{1,0:T(8,128)} fusion(f32[768,768]{1,0:T(8,128)S(1)} %get-tuple-element.8, f32[768,768]{1,0:T(8,128)} %collective-permute-done.5), kind=kOutput, calls=%fused_computation.107 | convolution fusion | flops 2717908992 | bytes 7077888 | tf_op jit(solution)/shard_map/dot_general | solution.py:46
  310.6 6.2 %fusion.72 = f32[768,768]{1,0:T(8,128)} fusion(f32[768,768]{1,0:T(8,128)S(1)} %copy-done.5, f32[768,768]{1,0:T(8,128)} %collective-permute-done.8), kind=kOutput, calls=%fused_computation.110 | convolution fusion | flops 2717908992 | bytes 7077888 | tf_op jit(solution)/shard_map/dot_general | solution.py:46
  316.8 6.5 %fusion.73 = f32[768,768]{1,0:T(8,128)} fusion(f32[768,768]{1,0:T(8,128)S(1)} %get-tuple-element.8, f32[768,768]{1,0:T(8,128)} %collective-permute-done.9), kind=kOutput, calls=%fused_computation.111 | convolution fusion | flops 2717908992 | bytes 7077888 | tf_op jit(solution)/shard_map/dot_general | solution.py:46
  341.6 8.4 %fusion.3 = f32[768,1536]{1,0:T(8,128)} fusion(f32[768,768]{1,0:T(8,128)S(1)} %get-tuple-element.6, f32[768,3072]{1,0:T(8,128)S(1)} %bitcast.94), kind=kOutput, calls=%fused_computation.21 | convolution fusion | flops 5435817984 | bytes 11796480 | tf_op jit(solution)/shard_map/dot_general | solution.py:46
  350.0 6.4 %fusion.1 = f32[768,1536]{1,0:T(8,128)S(1)} fusion(f32[768,768]{1,0:T(8,128)S(1)} %get-tuple-element.5, f32[768,3072]{1,0:T(8,128)S(1)} %bitcast.95), kind=kOutput, calls=%fused_computation.19 | convolution fusion | flops 5435817984 | bytes 11796480 | tf_op jit(solution)/shard_map/dot_general | solution.py:46
  356.4 8.1 %fusion.5 = f32[768,1536]{1,0:T(8,128)} fusion(f32[768,768]{1,0:T(8,128)S(1)} %get-tuple-element.4, f32[768,3072]{1,0:T(8,128)S(1)} %bitcast.96), kind=kOutput, calls=%fused_computation.23 | convolution fusion | flops 5435817984 | bytes 11796480 | tf_op jit(solution)/shard_map/dot_general | solution.py:46
  367.8 6.9 %fusion.34 = (f32[768,768]{1,0:T(8,128)}, f32[768,768]{1,0:T(8,128)}) fusion(f32[768,768]{1,0:T(8,128)} %copy-done.23, f32[768,1536]{1,0:T(8,128)} %fusion.3, pred[]{:T(512)S(6)} %le.28, f32[768,768]{1,0:T(8,128)} %collective-permute-done.10), kind=kLoop, calls=%fused_computation.57 | loop fusion | flops 2359296 | bytes 14155777 | tf_op jit(solution)/shard_map/add | solution.py:139
  374.7 5.8 %collective-permute-start.12 = (f32[768,768]{1,0:T(8,128)}, f32[768,768]{1,0:T(8,128)}, u32[]{:S(2)}, u32[]{:S(2)}) collective-permute-start(f32[768,768]{1,0:T(8,128)} %get-tuple-element.13), channel_id=1, source_target_pairs={{0,4},{4,8},{8,12},{1,5},{5,9},{9,13},{2,6},{6,10},{10,14},{3,7},{... | collective-permute-start | bytes 7077896 | tf_op jit(solution)/shard_map/ppermute | solution.py:140
  384.2 9.0 %collective-permute-done.11 = f32[768,768]{1,0:T(8,128)} collective-permute-done((f32[768,768]{1,0:T(8,128)}, f32[768,768]{1,0:T(8,128)}, u32[]{:S(2)}, u32[]{:S(2)}) %collective-permute-start.11) | collective-permute-done | bytes 2359328 | tf_op jit(solution)/shard_map/ppermute | solution.py:140
  393.2 5.3 fusion.33
  405.8 6.3 %fusion.58 = f32[768,768]{1,0:T(8,128)} fusion(f32[768,768]{1,0:T(8,128)} %collective-permute-done.10, s32[]{:T(128)S(6)} %select_n.333, f32[2,768,768]{2,1,0:T(8,128)S(1)} %bitcast.75, f32[2,768,768]{2,1,0:T(8,128)S(1)} %bitcast.82), kind=kOutput, calls=%fused_computation.100 | convolution fusion | flops 2718498816 | bytes 14155780 | tf_op jit(solution)/shard_map/dot_general | solution.py:46
  412.1 7.8 %add_negate_fusion.1 = f32[768,768]{1,0:T(8,128)} fusion(f32[768,768]{1,0:T(8,128)} %fusion.60, f32[768,768]{1,0:T(8,128)} %fusion.69, f32[768,768]{1,0:T(8,128)} %fusion.68, f32[768,768]{1,0:T(8,128)} %fusion.67, f32[768,768]{1,0:T(8,128)S(1)} %copy-done.7, f32[768,768]{1,0:T(8,128)} %fusion.66, f32[768,768]{1,0:T(8,128)} %collective-permute-done.7, ...), kind=kOutput, calls=%fused_computation.80 | convolution fusion | flops 2726166528 | bytes 28311562 | tf_op jit(solution)/shard_map/dot_general | solution.py:46
  420.0 6.4 %add_negate_fusion = f32[768,768]{1,0:T(8,128)S(1)} fusion(f32[768,768]{1,0:T(8,128)} %fusion.58, f32[768,768]{1,0:T(8,128)S(1)} %copy-done.9, f32[768,768]{1,0:T(8,128)S(1)} %copy-done.8, f32[768,768]{1,0:T(8,128)} %fusion.71, f32[768,768]{1,0:T(8,128)S(1)} %copy-done.6, f32[768,768]{1,0:T(8,128)} %fusion.70, f32[768,768]{1,0:T(8,128)} %collective-permute-done.11, ...), kind=kOutput, calls=%fused_computation.79 | convolution fusion | flops 2726166528 | bytes 28311562 | tf_op jit(solution)/shard_map/dot_general | solution.py:46
  431.1 46.4 %collective-permute-done.14 = f32[768,768]{1,0:T(8,128)} collective-permute-done((f32[768,768]{1,0:T(8,128)}, f32[768,768]{1,0:T(8,128)}, u32[]{:S(2)}, u32[]{:S(2)}) %collective-permute-start.14) | collective-permute-done | bytes 2359328 | tf_op jit(solution)/shard_map/ppermute | solution.py:140
  477.4 23.5 %collective-permute-done.15 = f32[768,768]{1,0:T(8,128)} collective-permute-done((f32[768,768]{1,0:T(8,128)}, f32[768,768]{1,0:T(8,128)}, u32[]{:S(2)}, u32[]{:S(2)}) %collective-permute-start.15) | collective-permute-done | bytes 2359328 | tf_op jit(solution)/shard_map/ppermute | solution.py:140
  500.9 6.0 %fusion.36 = (f32[768,768]{1,0:T(8,128)S(1)}, f32[768,768]{1,0:T(8,128)S(1)}) fusion(f32[768,768]{1,0:T(8,128)} %collective-permute-done.13, f32[768,768]{1,0:T(8,128)} %collective-permute-done.12, f32[768,1536]{1,0:T(8,128)} %fusion.5, f32[768,768]{1,0:T(8,128)} %collective-permute-done.15, f32[768,768]{1,0:T(8,128)} %collective-permute-done.14), kind=kLoop, calls=%fused_computation.60 | loop fusion | flops 3538944 | bytes 18874368 | tf_op jit(solution)/shard_map/neg | solution.py:144
  511.3 16.7 %psum.7 = f32[3072]{0:T(1024)S(1)} all-reduce(f32[3072]{0:T(1024)S(1)} %get-tuple-element.2), channel_id=1, replica_groups=mesh['parts'=2,'wide'=4,'col'=2,'sub'=2] {'wide'}, use_global_device_ids=true, to_apply=%region_1.2 | all-reduce | flops 3072 | bytes 24576 | tf_op jit(solution)/shard_map/psum | solution.py:147
  (126 shorter events, 109.8 us)
Async XLA Ops:
  7.2 136.1 %all-gather.5.cloned.1.call-start = ((), (), s32[]{:S(2)}) async-start(), calls=%async_computation | async-start | bytes 7077888 | tf_op jit(solution)/shard_map/all_gather | solution.py:114
  29.8 176.4 %all-gather.7.cloned.1.call-start = ((), (), s32[]{:S(2)}) async-start(), calls=%async_computation.1 | async-start | bytes 7077888 | tf_op jit(solution)/shard_map/all_gather | solution.py:114
  29.9 56.9 %collective-permute-start = (f32[768,768]{1,0:T(8,128)}, f32[768,768]{1,0:T(8,128)S(1)}, u32[]{:S(2)}, u32[]{:S(2)}) collective-permute-start(f32[768,768]{1,0:T(8,128)} %copy-done.2), channel_id=1, source_target_pairs={{0,4},{4,8},{8,12},{1,5},{5,9},{9,13},{2,6},{6,10},{10,14},{3,7},{... | collective-permute-start | bytes 7077896 | tf_op jit(solution)/shard_map/ppermute | solution.py:77
  34.9 56.3 %collective-permute-start.1 = (f32[768,768]{1,0:T(8,128)}, f32[768,768]{1,0:T(8,128)S(1)}, u32[]{:S(2)}, u32[]{:S(2)}) collective-permute-start(f32[768,768]{1,0:T(8,128)} %copy-done.2), channel_id=1, source_target_pairs={{4,0},{8,4},{12,8},{5,1},{9,5},{13,9},{6,2},{10,6},{14,10},{7,3},{... | collective-permute-start | bytes 7077896 | tf_op jit(solution)/shard_map/ppermute | solution.py:77
  36.2 99.8 %collective-permute-start.2 = (f32[768,768]{1,0:T(8,128)S(1)}, f32[768,768]{1,0:T(8,128)S(1)}, u32[]{:S(2)}, u32[]{:S(2)}) collective-permute-start(f32[768,768]{1,0:T(8,128)S(1)} %get-tuple-element.10.rest_1_), channel_id=1, source_target_pairs={{0,4},{4,8},{8,12},{1,5},{5,9},{9,13},{2,6},{6,10},{10,14},{3,7},{... | collective-permute-start | bytes 7077896 | tf_op jit(solution)/shard_map/ppermute | solution.py:77
  40.9 99.4 %collective-permute-start.3 = (f32[768,768]{1,0:T(8,128)S(1)}, f32[768,768]{1,0:T(8,128)S(1)}, u32[]{:S(2)}, u32[]{:S(2)}) collective-permute-start(f32[768,768]{1,0:T(8,128)S(1)} %get-tuple-element.10.rest_1_), channel_id=1, source_target_pairs={{4,0},{8,4},{12,8},{5,1},{9,5},{13,9},{6,2},{10,6},{14,10},{7,3},{... | collective-permute-start | bytes 7077896 | tf_op jit(solution)/shard_map/ppermute | solution.py:77
  86.7 54.1 %copy-start.14 = (f32[768,768]{1,0:T(8,128)}, f32[768,768]{1,0:T(8,128)S(1)}, u32[]{:S(2)}) copy-start(f32[768,768]{1,0:T(8,128)S(1)} %collective-permute-done) | copy-start | bytes 7077892
  91.2 49.1 %copy-start.11 = (f32[768,768]{1,0:T(8,128)}, f32[768,768]{1,0:T(8,128)S(1)}, u32[]{:S(2)}) copy-start(f32[768,768]{1,0:T(8,128)S(1)} %collective-permute-done.1) | copy-start | bytes 7077892
  155.6 66.5 %collective-permute-start.4 = (f32[768,768]{1,0:T(8,128)}, f32[768,768]{1,0:T(8,128)}, u32[]{:S(2)}, u32[]{:S(2)}) collective-permute-start(f32[768,768]{1,0:T(8,128)} %get-tuple-element.17), channel_id=1, source_target_pairs={{0,4},{4,8},{8,12},{1,5},{5,9},{9,13},{2,6},{6,10},{10,14},{3,7},{... | collective-permute-start | bytes 7077896 | tf_op jit(solution)/shard_map/ppermute | solution.py:140
  160.4 98.7 %collective-permute-start.8 = (f32[768,768]{1,0:T(8,128)}, f32[768,768]{1,0:T(8,128)}, u32[]{:S(2)}, u32[]{:S(2)}) collective-permute-start(f32[768,768]{1,0:T(8,128)} %get-tuple-element.18), channel_id=1, source_target_pairs={{0,4},{4,8},{8,12},{1,5},{5,9},{9,13},{2,6},{6,10},{10,14},{3,7},{... | collective-permute-start | bytes 7077896 | tf_op jit(solution)/shard_map/ppermute | solution.py:140
  164.4 9.5 %copy-start.12 = (f32[768,768]{1,0:T(8,128)S(1)}, f32[768,768]{1,0:T(8,128)}, u32[]{:S(2)}) copy-start(f32[768,768]{1,0:T(8,128)} %copy-done.11) | copy-start | bytes 7077892
  176.6 108.2 %collective-permute-start.5 = (f32[768,768]{1,0:T(8,128)}, f32[768,768]{1,0:T(8,128)}, u32[]{:S(2)}, u32[]{:S(2)}) collective-permute-start(f32[768,768]{1,0:T(8,128)} %get-tuple-element.23), channel_id=1, source_target_pairs={{4,0},{8,4},{12,8},{5,1},{9,5},{13,9},{6,2},{10,6},{14,10},{7,3},{... | collective-permute-start | bytes 7077896 | tf_op jit(solution)/shard_map/ppermute | solution.py:140
  177.9 106.9 %collective-permute-start.9 = (f32[768,768]{1,0:T(8,128)}, f32[768,768]{1,0:T(8,128)}, u32[]{:S(2)}, u32[]{:S(2)}) collective-permute-start(f32[768,768]{1,0:T(8,128)} %get-tuple-element.24), channel_id=1, source_target_pairs={{4,0},{8,4},{12,8},{5,1},{9,5},{13,9},{6,2},{10,6},{14,10},{7,3},{... | collective-permute-start | bytes 7077896 | tf_op jit(solution)/shard_map/ppermute | solution.py:140
  213.1 55.7 %slice-start.4 = ((s8[9437184]{0:T(1024)(128)(4,1)}), s8[4194304]{0:T(1024)(128)(4,1)S(1)}, s32[]{:S(2)}) async-start(s8[9437184]{0:T(1024)(128)(4,1)} %bitcast.89), calls=%async_computation.6 | async-start | bytes 8388608
  213.1 55.7 %slice-start.5 = ((s8[9437184]{0:T(1024)(128)(4,1)}), s8[4194304]{0:T(1024)(128)(4,1)S(1)}, s32[]{:S(2)}) async-start(s8[9437184]{0:T(1024)(128)(4,1)} %bitcast.89), calls=%async_computation.7 | async-start | bytes 8388608
  222.1 46.7 %slice-start.6 = ((s8[9437184]{0:T(1024)(128)(4,1)}), s8[1048576]{0:T(1024)(128)(4,1)S(1)}, s32[]{:S(2)}) async-start(s8[9437184]{0:T(1024)(128)(4,1)} %bitcast.89), calls=%async_computation.8 | async-start | bytes 2097152
  264.1 100.5 %collective-permute-start.6 = (f32[768,768]{1,0:T(8,128)}, f32[768,768]{1,0:T(8,128)S(1)}, u32[]{:S(2)}, u32[]{:S(2)}) collective-permute-start(f32[768,768]{1,0:T(8,128)} %get-tuple-element.15), channel_id=1, source_target_pairs={{0,4},{4,8},{8,12},{1,5},{5,9},{9,13},{2,6},{6,10},{10,14},{3,7},{... | collective-permute-start | bytes 7077896 | tf_op jit(solution)/shard_map/ppermute | solution.py:140
  289.8 94.4 %collective-permute-start.7 = (f32[768,768]{1,0:T(8,128)}, f32[768,768]{1,0:T(8,128)}, u32[]{:S(2)}, u32[]{:S(2)}) collective-permute-start(f32[768,768]{1,0:T(8,128)} %get-tuple-element.21), channel_id=1, source_target_pairs={{4,0},{8,4},{12,8},{5,1},{9,5},{13,9},{6,2},{10,6},{14,10},{7,3},{... | collective-permute-start | bytes 7077896 | tf_op jit(solution)/shard_map/ppermute | solution.py:140
  291.1 76.7 %collective-permute-start.10 = (f32[768,768]{1,0:T(8,128)}, f32[768,768]{1,0:T(8,128)}, u32[]{:S(2)}, u32[]{:S(2)}) collective-permute-start(f32[768,768]{1,0:T(8,128)} %get-tuple-element.16), channel_id=1, source_target_pairs={{0,4},{4,8},{8,12},{1,5},{5,9},{9,13},{2,6},{6,10},{10,14},{3,7},{... | collective-permute-start | bytes 7077896 | tf_op jit(solution)/shard_map/ppermute | solution.py:140
  297.1 96.1 %collective-permute-start.11 = (f32[768,768]{1,0:T(8,128)}, f32[768,768]{1,0:T(8,128)}, u32[]{:S(2)}, u32[]{:S(2)}) collective-permute-start(f32[768,768]{1,0:T(8,128)} %get-tuple-element.22), channel_id=1, source_target_pairs={{4,0},{8,4},{12,8},{5,1},{9,5},{13,9},{6,2},{10,6},{14,10},{7,3},{... | collective-permute-start | bytes 7077896 | tf_op jit(solution)/shard_map/ppermute | solution.py:140
  367.8 33.3 %slice-start = ((s8[4718592]{0:T(1024)(128)(4,1)}), s8[4194304]{0:T(1024)(128)(4,1)S(1)}, s32[]{:S(2)}) async-start(s8[4718592]{0:T(1024)(128)(4,1)} %bitcast.72), calls=%async_computation.2 | async-start | bytes 8388608
  367.8 33.3 %slice-start.2 = ((s8[4718592]{0:T(1024)(128)(4,1)}), s8[4194304]{0:T(1024)(128)(4,1)S(1)}, s32[]{:S(2)}) async-start(s8[4718592]{0:T(1024)(128)(4,1)} %bitcast.79), calls=%async_computation.4 | async-start | bytes 8388608
  374.7 56.4 %collective-permute-start.12 = (f32[768,768]{1,0:T(8,128)}, f32[768,768]{1,0:T(8,128)}, u32[]{:S(2)}, u32[]{:S(2)}) collective-permute-start(f32[768,768]{1,0:T(8,128)} %get-tuple-element.13), channel_id=1, source_target_pairs={{0,4},{4,8},{8,12},{1,5},{5,9},{9,13},{2,6},{6,10},{10,14},{3,7},{... | collective-permute-start | bytes 7077896 | tf_op jit(solution)/shard_map/ppermute | solution.py:140
  380.5 20.6 %slice-start.1 = ((s8[4718592]{0:T(1024)(128)(4,1)}), s8[524288]{0:T(1024)(128)(4,1)S(1)}, s32[]{:S(2)}) async-start(s8[4718592]{0:T(1024)(128)(4,1)} %bitcast.72), calls=%async_computation.3 | async-start | bytes 1048576
  380.5 20.6 %slice-start.3 = ((s8[4718592]{0:T(1024)(128)(4,1)}), s8[524288]{0:T(1024)(128)(4,1)S(1)}, s32[]{:S(2)}) async-start(s8[4718592]{0:T(1024)(128)(4,1)} %bitcast.79), calls=%async_computation.5 | async-start | bytes 1048576
  380.5 20.6 %copy-start.24 = (f32[768,768]{1,0:T(8,128)S(1)}, f32[768,768]{1,0:T(8,128)}, u32[]{:S(2)}) copy-start(f32[768,768]{1,0:T(8,128)} %copy-done.23) | copy-start | bytes 7077892
  380.5 96.9 %collective-permute-start.14 = (f32[768,768]{1,0:T(8,128)}, f32[768,768]{1,0:T(8,128)}, u32[]{:S(2)}, u32[]{:S(2)}) collective-permute-start(f32[768,768]{1,0:T(8,128)} %get-tuple-element.14), channel_id=1, source_target_pairs={{0,4},{4,8},{8,12},{1,5},{5,9},{9,13},{2,6},{6,10},{10,14},{3,7},{... | collective-permute-start | bytes 7077896 | tf_op jit(solution)/shard_map/ppermute | solution.py:140
  398.5 79.0 %collective-permute-start.13 = (f32[768,768]{1,0:T(8,128)}, f32[768,768]{1,0:T(8,128)}, u32[]{:S(2)}, u32[]{:S(2)}) collective-permute-start(f32[768,768]{1,0:T(8,128)} %get-tuple-element.19), channel_id=1, source_target_pairs={{4,0},{8,4},{12,8},{5,1},{9,5},{13,9},{6,2},{10,6},{14,10},{7,3},{... | collective-permute-start | bytes 7077896 | tf_op jit(solution)/shard_map/ppermute | solution.py:140
  399.8 101.2 %collective-permute-start.15 = (f32[768,768]{1,0:T(8,128)}, f32[768,768]{1,0:T(8,128)}, u32[]{:S(2)}, u32[]{:S(2)}) collective-permute-start(f32[768,768]{1,0:T(8,128)} %get-tuple-element.20), channel_id=1, source_target_pairs={{4,0},{8,4},{12,8},{5,1},{9,5},{13,9},{6,2},{10,6},{14,10},{7,3},{... | collective-permute-start | bytes 7077896 | tf_op jit(solution)/shard_map/ppermute | solution.py:140
  426.4 80.6 %copy-start.10 = (f32[768,768]{1,0:T(8,128)S(1)}, f32[768,768]{1,0:T(8,128)}, u32[]{:S(2)}) copy-start(f32[768,768]{1,0:T(8,128)} %add_negate_fusion.1) | copy-start | bytes 7077892
  506.9 21.1 %copy-start.25 = (f32[1,3072]{1,0:T(1,128)S(1)}, f32[1,3072]{1,0:T(1,128)}, u32[]{:S(2)}) copy-start(f32[1,3072]{1,0:T(1,128)} %param.9) | copy-start | bytes 36868
  507.0 21.7 %copy-start.1 = (s32[1,4]{1,0:T(1,128)S(1)}, s32[1,4]{1,0:T(1,128)}, u32[]{:S(2)}) copy-start(s32[1,4]{1,0:T(1,128)} %param.7) | copy-start | bytes 52
  (19 other events, 98.7 us)
Sparse Core Ops, SparseCore 0:
  29.9 65.3 all-gather.4
  143.4 62.7 all-gather.6

commit v3 on v2

--- a/solution.py
+++ b/solution.py
@@ -107,10 +107,6 @@
             parent_inverse,
             *spread,
         )
-        if i == 1:
-            corner = sum(jnp.abs(x[0, 0]) for pair in got for x in pair)
-            corner = jnp.minimum(corner.astype(jnp.int32), 0)
-            local = jnp.where(corner >= 0, local, 0.0)
         pieces.append(lax.all_gather(local, "col", axis=0))
     blocks = jnp.concatenate(pieces, axis=0)
 
@@ -132,10 +128,9 @@
                 away = lax.dynamic_index_in_dim(pieces[0], owner, 0, keepdims=False)
             else:
                 away = sigma(target)
-            terms = dot(away, summed, ((0,), (0,)))
             for p in range(PIPES):
                 came = got[p][w]
-                term = terms[:, p * pipe : (p + 1) * pipe]
+                term = dot(away, summed[:, p * pipe : (p + 1) * pipe], ((0,), (0,)))
                 send = flat(came + jnp.where(rank <= step - 2, term, 0.0))
                 got[p][w] = flat(lax.ppermute(send, "wide", perm))
                 total[p] += jnp.where(rank >= step - 1, dot(here, came, ((1,), (0,))), 0.0)

time: 544 us -> 520 us (0.956)
  other arithmetic: 49.3 us -> 23.1 us
  waiting for transfers between devices: 230 us -> 205 us
  matrix products: 135 us -> 158 us
  starting transfers between devices: 49 us -> 57.1 us
    add x6 -> x0, other arithmetic: 27.7 us -> none  [per_device(): send = flat(came + jnp.where(rank <= step - 2, term, 0.0))]
    all_gather x2, waiting for transfers between devices: 27 us -> 0.02 us  [per_device(): pieces.append(lax.all_gather(local, 'col', axis=0))]
    dot_general x21 -> x27, matrix products: 135 us -> 158 us  [dot(): lax.dot_general(a, b, ((contract[0], contract[1]), ((), ())), precision=l...]
    ppermute x12, waiting for transfers between devices: 122 us -> 136 us  [per_device(): got[p][w] = flat(lax.ppermute(send, 'wide', perm))]
    ppermute x4, waiting for transfers between devices: 80.2 us -> 69.4 us  [per_device(): lax.ppermute(spread[p], 'wide', perm)]
  transfers between devices with their start and end apart: 18 -> 18, of which waited for: 11 -> 8; matrix products, arithmetic and copies ran while one was open for 32% -> 32% of each run, Pallas kernels for 2% -> 2%
where the time goes in v3:
time: 520 us; the launch traced here: 510 us
  waiting for transfers between devices  205 us (39%)
  matrix products  158 us (30%)
  starting transfers between devices  57.1 us (11%)
  Pallas kernels  24.5 us (5%)
  other arithmetic  23.1 us (4%)
  blocking collectives  15.6 us (3%)
  between operations  15 us (3%)
  local copies, waits for them, and re-layouts  12.2 us (2%)
    dot_general x27, matrix products, dot(): lax.dot_general(a, b, ((contract[0], contract[1]), ((), ())), precision=l...  158 us
    ppermute x12, waiting for transfers between devices, per_device(): got[p][w] = flat(lax.ppermute(send, 'wide', perm))  136 us
    ppermute x4, waiting for transfers between devices, per_device(): lax.ppermute(spread[p], 'wide', perm)  69.4 us
    ppermute x12, starting transfers between devices, per_device(): got[p][w] = flat(lax.ppermute(send, 'wide', perm))  41.9 us
    pallas_call x2, Pallas kernels, per_device(): pl.pallas_call(pick_kernel, out_shape=jax.ShapeDtypeStruct((slots, slots)...  24.5 us
    psum x1, blocking collectives, per_device(): totals = lax.psum(partial_value, 'wide')  15.6 us
    ppermute x4, starting transfers between devices, per_device(): lax.ppermute(spread[p], 'wide', perm)  15 us
  transfers between devices with their start and end apart: 18, of which 8 were waited for; matrix products, arithmetic and copies ran while one was open for 32% of the time, Pallas kernels for 2%

profile of v3, /device:TPU:0, one launch (start us, length us, event | category | flops | bytes accessed | tf_op | source)
XLA Modules:
  0.0 510.4 jit_solution(17634262864529287862)
XLA Ops:
  14.5 12.3 %pick.2 = f32[768,768]{1,0:T(8,128)S(1)} custom-call(s32[1]{0:T(128)} %bitcast.at_ref, s32[768]{0:T(1024)S(1)} %get-tuple-element.15.mine_ref, f32[768,1]{1,0:T(8,128)S(1)} %fusion.61.live_ref, s32[1,768]{1,0:T(1,128)S(1)} %get-tuple-element.14.wanted_ref, f32[2048,4096]{1,0:T(8,128)} %parent_ref.3, f32[768,768]{1,0:T(8,128)S(1)} %get-tuple-element.9.rest_0_, ...), custom_call_target="tpu_custom_call" | custom-call | flops 1000 | bytes 1000 | tf_op jit(solution)/shard_map/pick/pallas_call | solution.py:87
  31.4 12.2 %pick.3 = f32[768,768]{1,0:T(8,128)S(1)} custom-call(s32[1]{0:T(128)} %bitcast.8.at_ref, s32[768]{0:T(1024)S(1)} %get-tuple-element.15.mine_ref, f32[768,1]{1,0:T(8,128)S(1)} %fusion.61.live_ref, s32[1,768]{1,0:T(1,128)S(1)} %get-tuple-element.13.wanted_ref, f32[2048,4096]{1,0:T(8,128)} %parent_ref.3, f32[768,768]{1,0:T(8,128)S(1)} %copy-done.3, ...), custom_call_target="tpu_custom_call" | custom-call | flops 1000 | bytes 1000 | tf_op jit(solution)/shard_map/pick/pallas_call | solution.py:87
  45.0 6.5 %collective-permute-start = (f32[768,768]{1,0:T(8,128)}, f32[768,768]{1,0:T(8,128)}, u32[]{:S(2)}, u32[]{:S(2)}) collective-permute-start(f32[768,768]{1,0:T(8,128)} %copy-done.2), channel_id=1, source_target_pairs={{0,4},{4,8},{8,12},{1,5},{5,9},{9,13},{2,6},{6,10},{10,14},{3,7},{... | collective-permute-start | bytes 7077896 | tf_op jit(solution)/shard_map/ppermute | solution.py:77
  52.8 6.0 %collective-permute-start.6 = (f32[768,768]{1,0:T(8,128)S(1)}, f32[768,768]{1,0:T(8,128)}, u32[]{:S(2)}, u32[]{:S(2)}) collective-permute-start(f32[768,768]{1,0:T(8,128)S(1)} %get-tuple-element.10.rest_1_), channel_id=1, source_target_pairs={{0,4},{4,8},{8,12},{1,5},{5,9},{9,13},{2,6},{6,10},{10,14},{3,7},{... | collective-permute-start | bytes 7077896 | tf_op jit(solution)/shard_map/ppermute | solution.py:77
  60.2 41.8 %collective-permute-done = f32[768,768]{1,0:T(8,128)} collective-permute-done((f32[768,768]{1,0:T(8,128)}, f32[768,768]{1,0:T(8,128)}, u32[]{:S(2)}, u32[]{:S(2)}) %collective-permute-start) | collective-permute-done | bytes 2359328 | tf_op jit(solution)/shard_map/ppermute | solution.py:77
  102.0 9.1 %select_add_fusion.11 = f32[768,768]{1,0:T(8,128)} fusion(f32[768,768]{1,0:T(8,128)} %collective-permute-done, f32[768,3072]{1,0:T(8,128)} %bitcast.85, f32[2,768,768]{2,1,0:T(8,128)} %bitcast.102, s32[]{:T(128)S(6)} %select_n.309, pred[]{:T(512)S(6)} %le.24), kind=kOutput, calls=%fused_computation.62 | convolution fusion | flops 2719088640 | bytes 9437189 | tf_op jit(solution)/shard_map/dot_general | solution.py:46
  116.9 6.6 %select_add_fusion.10 = f32[768,768]{1,0:T(8,128)} fusion(f32[768,768]{1,0:T(8,128)} %collective-permute-done.1, f32[768,3072]{1,0:T(8,128)} %bitcast.86, f32[2,768,768]{2,1,0:T(8,128)S(1)} %bitcast.105, s32[]{:T(128)S(6)} %select_n.319, pred[]{:T(512)S(6)} %le.25), kind=kOutput, calls=%fused_computation.61 | convolution fusion | flops 2719088640 | bytes 9437189 | tf_op jit(solution)/shard_map/dot_general | solution.py:46
  124.8 27.6 %collective-permute-done.6 = f32[768,768]{1,0:T(8,128)} collective-permute-done((f32[768,768]{1,0:T(8,128)S(1)}, f32[768,768]{1,0:T(8,128)}, u32[]{:S(2)}, u32[]{:S(2)}) %collective-permute-start.6) | collective-permute-done | bytes 2359328 | tf_op jit(solution)/shard_map/ppermute | solution.py:77
  152.5 6.7 %select_add_fusion.7 = f32[768,768]{1,0:T(8,128)} fusion(f32[768,768]{1,0:T(8,128)} %collective-permute-done.6, f32[768,3072]{1,0:T(8,128)} %bitcast.87, f32[2,768,768]{2,1,0:T(8,128)S(1)} %bitcast.106, s32[]{:T(128)S(6)} %select_n.309, pred[]{:T(512)S(6)} %le.24), kind=kOutput, calls=%fused_computation.57 | convolution fusion | flops 2719088640 | bytes 9437189 | tf_op jit(solution)/shard_map/dot_general | solution.py:46
  159.2 6.1 %collective-permute-start.8 = (f32[768,768]{1,0:T(8,128)}, f32[768,768]{1,0:T(8,128)}, u32[]{:S(2)}, u32[]{:S(2)}) collective-permute-start(f32[768,768]{1,0:T(8,128)} %select_add_fusion.7), channel_id=1, source_target_pairs={{0,4},{4,8},{8,12},{1,5},{5,9},{9,13},{2,6},{6,10},{10,14},{3,7},{... | collective-permute-start | bytes 7077896 | tf_op jit(solution)/shard_map/ppermute | solution.py:135
  165.4 7.3 %fusion.6 = (f32[768,768]{1,0:T(8,128)}, f32[768,768]{1,0:T(8,128)S(1)}, f32[768,768]{1,0:T(8,128)S(1)}, f32[768,768]{1,0:T(8,128)S(1)}, f32[768,768]{1,0:T(8,128)}) fusion(s32[]{:T(128)S(6)} %select_n.289, f32[2,768,768]{2,1,0:T(8,128)} %bitcast.103, f32[2,768,768]{2,1,0:T(8,128)} %bitcast.113, s32[]{:T(128)S(6)} %select_n.294, s32[]{:T(128)S(6)} %select_n.300, ...), kind=kLoop, calls=%fused_computation.24 | loop fusion | flops 2949120 | bytes 21233684 | tf_op jit(solution)/shard_map/jit(dynamic_index_in_dim)/squeeze | solution.py:117
  174.0 6.3 %fusion.70 = f32[768,768]{1,0:T(8,128)} fusion(f32[768,768]{1,0:T(8,128)} %get-tuple-element.4, f32[768,3072]{1,0:T(8,128)S(1)} %bitcast.90), kind=kOutput, calls=%fused_computation.95 | convolution fusion | flops 2717908992 | bytes 7077888 | tf_op jit(solution)/shard_map/dot_general | solution.py:46
  192.2 6.1 %fusion.80 = f32[768,768]{1,0:T(8,128)} fusion(f32[768,768]{1,0:T(8,128)S(1)} %get-tuple-element.5, f32[768,768]{1,0:T(8,128)} %collective-permute-done), kind=kOutput, calls=%fused_computation.101 | convolution fusion | flops 2717908992 | bytes 7077888 | tf_op jit(solution)/shard_map/dot_general | solution.py:46
  198.3 6.1 %fusion.84 = f32[768,768]{1,0:T(8,128)} fusion(f32[768,768]{1,0:T(8,128)S(1)} %get-tuple-element.5, f32[768,768]{1,0:T(8,128)} %collective-permute-done.6), kind=kOutput, calls=%fused_computation.105 | convolution fusion | flops 2717908992 | bytes 7077888 | tf_op jit(solution)/shard_map/dot_general | solution.py:46
  204.5 6.2 %fusion.81 = f32[768,768]{1,0:T(8,128)} fusion(f32[768,768]{1,0:T(8,128)S(1)} %get-tuple-element.6, f32[768,768]{1,0:T(8,128)} %collective-permute-done.1), kind=kOutput, calls=%fused_computation.102 | convolution fusion | flops 2717908992 | bytes 7077888 | tf_op jit(solution)/shard_map/dot_general | solution.py:46
  210.6 6.3 %fusion.85 = f32[768,768]{1,0:T(8,128)} fusion(f32[768,768]{1,0:T(8,128)S(1)} %get-tuple-element.6, f32[768,768]{1,0:T(8,128)} %collective-permute-done.7), kind=kOutput, calls=%fused_computation.106 | convolution fusion | flops 2717908992 | bytes 7077888 | tf_op jit(solution)/shard_map/dot_general | solution.py:46
  216.9 7.5 %fusion.1 = f32[768,1536]{1,0:T(8,128)} fusion(f32[768,768]{1,0:T(8,128)S(1)} %copy-done.8, f32[768,3072]{1,0:T(8,128)S(1)} %bitcast.93), kind=kOutput, calls=%fused_computation.19 | convolution fusion | flops 5435817984 | bytes 11796480 | tf_op jit(solution)/shard_map/dot_general | solution.py:46
  234.2 19.4 %collective-permute-done.8 = f32[768,768]{1,0:T(8,128)} collective-permute-done((f32[768,768]{1,0:T(8,128)}, f32[768,768]{1,0:T(8,128)}, u32[]{:S(2)}, u32[]{:S(2)}) %collective-permute-start.8) | collective-permute-done | bytes 2359328 | tf_op jit(solution)/shard_map/ppermute | solution.py:135
  268.1 5.9 %select_add_fusion.8 = f32[768,768]{1,0:T(8,128)} fusion(f32[768,768]{1,0:T(8,128)} %collective-permute-done.3, f32[768,768]{1,0:T(8,128)S(1)} %get-tuple-element.7, f32[768,3072]{1,0:T(8,128)S(1)} %bitcast.97, pred[]{:T(512)S(6)} %le.27), kind=kOutput, calls=%fused_computation.59 | convolution fusion | flops 2719088640 | bytes 9437185 | tf_op jit(solution)/shard_map/dot_general | solution.py:46
  275.7 6.1 %fusion.82 = f32[768,768]{1,0:T(8,128)} fusion(f32[768,768]{1,0:T(8,128)S(1)} %get-tuple-element.7, f32[768,768]{1,0:T(8,128)} %collective-permute-done.2), kind=kOutput, calls=%fused_computation.103 | convolution fusion | flops 2717908992 | bytes 7077888 | tf_op jit(solution)/shard_map/dot_general | solution.py:46
  281.8 6.1 %fusion.83 = f32[768,768]{1,0:T(8,128)} fusion(f32[768,768]{1,0:T(8,128)S(1)} %copy-done.7, f32[768,768]{1,0:T(8,128)} %collective-permute-done.3), kind=kOutput, calls=%fused_computation.104 | convolution fusion | flops 2717908992 | bytes 7077888 | tf_op jit(solution)/shard_map/dot_general | solution.py:46
  292.3 6.3 %fusion.86 = f32[768,768]{1,0:T(8,128)} fusion(f32[768,768]{1,0:T(8,128)S(1)} %get-tuple-element.7, f32[768,768]{1,0:T(8,128)} %collective-permute-done.8), kind=kOutput, calls=%fused_computation.107 | convolution fusion | flops 2717908992 | bytes 7077888 | tf_op jit(solution)/shard_map/dot_general | solution.py:46
  298.7 54.9 %collective-permute-done.10 = f32[768,768]{1,0:T(8,128)S(1)} collective-permute-done((f32[768,768]{1,0:T(8,128)S(1)}, f32[768,768]{1,0:T(8,128)S(1)}, u32[]{:S(2)}, u32[]{:S(2)}) %collective-permute-start.10) | collective-permute-done | bytes 2359328 | tf_op jit(solution)/shard_map/ppermute | solution.py:135
  358.5 5.8 %collective-permute-start.14 = (f32[768,768]{1,0:T(8,128)}, f32[768,768]{1,0:T(8,128)}, u32[]{:S(2)}, u32[]{:S(2)}) collective-permute-start(f32[768,768]{1,0:T(8,128)} %select_add_fusion.1), channel_id=1, source_target_pairs={{0,4},{4,8},{8,12},{1,5},{5,9},{9,13},{2,6},{6,10},{10,14},{3,7},{... | collective-permute-start | bytes 7077896 | tf_op jit(solution)/shard_map/ppermute | solution.py:135
  375.7 6.1 %collective-permute-start.12 = (f32[768,768]{1,0:T(8,128)}, f32[768,768]{1,0:T(8,128)}, u32[]{:S(2)}, u32[]{:S(2)}) collective-permute-start(f32[768,768]{1,0:T(8,128)} %select_add_fusion.3), channel_id=1, source_target_pairs={{0,4},{4,8},{8,12},{1,5},{5,9},{9,13},{2,6},{6,10},{10,14},{3,7},{... | collective-permute-start | bytes 7077896 | tf_op jit(solution)/shard_map/ppermute | solution.py:135
  397.6 7.6 %add_negate_fusion.1 = f32[768,768]{1,0:T(8,128)} fusion(f32[768,768]{1,0:T(8,128)} %fusion.74, f32[768,768]{1,0:T(8,128)} %fusion.83, f32[768,768]{1,0:T(8,128)} %fusion.82, f32[768,768]{1,0:T(8,128)} %fusion.81, f32[768,768]{1,0:T(8,128)S(1)} %copy-done.11, f32[768,768]{1,0:T(8,128)} %fusion.80, f32[768,768]{1,0:T(8,128)} %copy-done.14, pred[]{:T(512)S(6)} %ge.29, ...), kind=kOutput, calls=%fused_computation.58 | convolution fusion | flops 2726166528 | bytes 28311562 | tf_op jit(solution)/shard_map/dot_general | solution.py:46
  405.2 7.2 %add_negate_fusion = f32[768,768]{1,0:T(8,128)} fusion(f32[768,768]{1,0:T(8,128)} %fusion.72, f32[768,768]{1,0:T(8,128)} %fusion.87, f32[768,768]{1,0:T(8,128)} %fusion.86, f32[768,768]{1,0:T(8,128)S(1)} %copy-done.12, f32[768,768]{1,0:T(8,128)S(1)} %copy-done.9, f32[768,768]{1,0:T(8,128)S(1)} %copy-done.10, f32[768,768]{1,0:T(8,128)} %copy-done.13, ...), kind=kOutput, calls=%fused_computation.53 | convolution fusion | flops 2726166528 | bytes 28311562 | tf_op jit(solution)/shard_map/dot_general | solution.py:46
  414.8 10.9 %collective-permute-done.15 = f32[768,768]{1,0:T(8,128)} collective-permute-done((f32[768,768]{1,0:T(8,128)}, f32[768,768]{1,0:T(8,128)}, u32[]{:S(2)}, u32[]{:S(2)}) %collective-permute-start.15) | collective-permute-done | bytes 2359328 | tf_op jit(solution)/shard_map/ppermute | solution.py:135
  425.8 37.5 %collective-permute-done.12 = f32[768,768]{1,0:T(8,128)} collective-permute-done((f32[768,768]{1,0:T(8,128)}, f32[768,768]{1,0:T(8,128)}, u32[]{:S(2)}, u32[]{:S(2)}) %collective-permute-start.12) | collective-permute-done | bytes 2359328 | tf_op jit(solution)/shard_map/ppermute | solution.py:135
  463.3 10.7 %collective-permute-done.13 = f32[768,768]{1,0:T(8,128)} collective-permute-done((f32[768,768]{1,0:T(8,128)}, f32[768,768]{1,0:T(8,128)}, u32[]{:S(2)}, u32[]{:S(2)}) %collective-permute-start.13) | collective-permute-done | bytes 2359328 | tf_op jit(solution)/shard_map/ppermute | solution.py:135
  474.0 7.5 %fusion.20 = (f32[768,768]{1,0:T(8,128)S(1)}, f32[768,768]{1,0:T(8,128)}) fusion(f32[768,768]{1,0:T(8,128)} %collective-permute-done.13, f32[768,768]{1,0:T(8,128)} %collective-permute-done.12, f32[768,1536]{1,0:T(8,128)} %fusion.1, f32[768,768]{1,0:T(8,128)} %collective-permute-done.15, f32[768,768]{1,0:T(8,128)} %collective-permute-done.14), kind=kLoop, calls=%fused_computation.40 | loop fusion | flops 3538944 | bytes 18874368 | tf_op jit(solution)/shard_map/neg | solution.py:139
  487.0 15.6 %psum.7 = f32[3072]{0:T(1024)S(1)} all-reduce(f32[3072]{0:T(1024)S(1)} %get-tuple-element.2), channel_id=1, replica_groups=mesh['parts'=2,'wide'=4,'col'=2,'sub'=2] {'wide'}, use_global_device_ids=true, to_apply=%region_1.2 | all-reduce | flops 3072 | bytes 24576 | tf_op jit(solution)/shard_map/psum | solution.py:142
  (105 shorter events, 106.9 us)
Async XLA Ops:
  7.2 94.8 %all-gather.5.cloned.1.call-start = ((), (), s32[]{:S(2)}) async-start(), calls=%async_computation | async-start | bytes 7077888 | tf_op jit(solution)/shard_map/all_gather | solution.py:110
  29.7 135.6 %all-gather.7.cloned.1.call-start = ((), (), s32[]{:S(2)}) async-start(), calls=%async_computation.1 | async-start | bytes 7077888 | tf_op jit(solution)/shard_map/all_gather | solution.py:110
  45.0 57.0 %collective-permute-start = (f32[768,768]{1,0:T(8,128)}, f32[768,768]{1,0:T(8,128)}, u32[]{:S(2)}, u32[]{:S(2)}) collective-permute-start(f32[768,768]{1,0:T(8,128)} %copy-done.2), channel_id=1, source_target_pairs={{0,4},{4,8},{8,12},{1,5},{5,9},{9,13},{2,6},{6,10},{10,14},{3,7},{... | collective-permute-start | bytes 7077896 | tf_op jit(solution)/shard_map/ppermute | solution.py:77
  51.5 65.4 %collective-permute-start.1 = (f32[768,768]{1,0:T(8,128)}, f32[768,768]{1,0:T(8,128)}, u32[]{:S(2)}, u32[]{:S(2)}) collective-permute-start(f32[768,768]{1,0:T(8,128)} %copy-done.2), channel_id=1, source_target_pairs={{4,0},{8,4},{12,8},{5,1},{9,5},{13,9},{6,2},{10,6},{14,10},{7,3},{... | collective-permute-start | bytes 7077896 | tf_op jit(solution)/shard_map/ppermute | solution.py:77
  52.8 99.7 %collective-permute-start.6 = (f32[768,768]{1,0:T(8,128)S(1)}, f32[768,768]{1,0:T(8,128)}, u32[]{:S(2)}, u32[]{:S(2)}) collective-permute-start(f32[768,768]{1,0:T(8,128)S(1)} %get-tuple-element.10.rest_1_), channel_id=1, source_target_pairs={{0,4},{4,8},{8,12},{1,5},{5,9},{9,13},{2,6},{6,10},{10,14},{3,7},{... | collective-permute-start | bytes 7077896 | tf_op jit(solution)/shard_map/ppermute | solution.py:77
  58.8 125.9 %collective-permute-start.7 = (f32[768,768]{1,0:T(8,128)S(1)}, f32[768,768]{1,0:T(8,128)}, u32[]{:S(2)}, u32[]{:S(2)}) collective-permute-start(f32[768,768]{1,0:T(8,128)S(1)} %get-tuple-element.10.rest_1_), channel_id=1, source_target_pairs={{4,0},{8,4},{12,8},{5,1},{9,5},{13,9},{6,2},{10,6},{14,10},{7,3},{... | collective-permute-start | bytes 7077896 | tf_op jit(solution)/shard_map/ppermute | solution.py:77
  102.0 14.9 %copy-start.6 = (f32[1536,768]{1,0:T(8,128)S(1)}, f32[1536,768]{1,0:T(8,128)}, u32[]{:S(2)}) copy-start(f32[1536,768]{1,0:T(8,128)} %all-gather.5.cloned.1.call-done) | copy-start | bytes 14155780
  111.1 113.4 %collective-permute-start.2 = (f32[768,768]{1,0:T(8,128)}, f32[768,768]{1,0:T(8,128)}, u32[]{:S(2)}, u32[]{:S(2)}) collective-permute-start(f32[768,768]{1,0:T(8,128)} %select_add_fusion.11), channel_id=1, source_target_pairs={{0,4},{4,8},{8,12},{1,5},{5,9},{9,13},{2,6},{6,10},{10,14},{3,7},{... | collective-permute-start | bytes 7077896 | tf_op jit(solution)/shard_map/ppermute | solution.py:135
  123.5 144.6 %collective-permute-start.3 = (f32[768,768]{1,0:T(8,128)}, f32[768,768]{1,0:T(8,128)}, u32[]{:S(2)}, u32[]{:S(2)}) collective-permute-start(f32[768,768]{1,0:T(8,128)} %select_add_fusion.10), channel_id=1, source_target_pairs={{4,0},{8,4},{12,8},{5,1},{9,5},{13,9},{6,2},{10,6},{14,10},{7,3},{... | collective-permute-start | bytes 7077896 | tf_op jit(solution)/shard_map/ppermute | solution.py:135
  152.5 20.2 %slice-start = ((s8[9437184]{0:T(1024)(128)(4,1)}), s8[1048576]{0:T(1024)(128)(4,1)S(1)}, s32[]{:S(2)}) async-start(s8[9437184]{0:T(1024)(128)(4,1)} %bitcast.88), calls=%async_computation.2 | async-start | bytes 2097152
  159.2 94.5 %collective-permute-start.8 = (f32[768,768]{1,0:T(8,128)}, f32[768,768]{1,0:T(8,128)}, u32[]{:S(2)}, u32[]{:S(2)}) collective-permute-start(f32[768,768]{1,0:T(8,128)} %select_add_fusion.7), channel_id=1, source_target_pairs={{0,4},{4,8},{8,12},{1,5},{5,9},{9,13},{2,6},{6,10},{10,14},{3,7},{... | collective-permute-start | bytes 7077896 | tf_op jit(solution)/shard_map/ppermute | solution.py:135
  165.4 8.6 %slice-start.2 = ((s8[9437184]{0:T(1024)(128)(4,1)}), s8[4194304]{0:T(1024)(128)(4,1)S(1)}, s32[]{:S(2)}) async-start(s8[9437184]{0:T(1024)(128)(4,1)} %bitcast.88), calls=%async_computation.4 | async-start | bytes 8388608
  190.4 72.8 %collective-permute-start.9 = (f32[768,768]{1,0:T(8,128)S(1)}, f32[768,768]{1,0:T(8,128)S(1)}, u32[]{:S(2)}, u32[]{:S(2)}) collective-permute-start(f32[768,768]{1,0:T(8,128)S(1)} %select_add_fusion.6), channel_id=1, source_target_pairs={{4,0},{8,4},{12,8},{5,1},{9,5},{13,9},{6,2},{10,6},{14,10},{7,3},{... | collective-permute-start | bytes 7077896 | tf_op jit(solution)/shard_map/ppermute | solution.py:135
  229.5 141.1 %collective-permute-start.4 = (f32[768,768]{1,0:T(8,128)S(1)}, f32[768,768]{1,0:T(8,128)S(1)}, u32[]{:S(2)}, u32[]{:S(2)}) collective-permute-start(f32[768,768]{1,0:T(8,128)S(1)} %select_add_fusion.9), channel_id=1, source_target_pairs={{0,4},{4,8},{8,12},{1,5},{5,9},{9,13},{2,6},{6,10},{10,14},{3,7},{... | collective-permute-start | bytes 7077896 | tf_op jit(solution)/shard_map/ppermute | solution.py:135
  258.7 94.8 %collective-permute-start.10 = (f32[768,768]{1,0:T(8,128)S(1)}, f32[768,768]{1,0:T(8,128)S(1)}, u32[]{:S(2)}, u32[]{:S(2)}) collective-permute-start(f32[768,768]{1,0:T(8,128)S(1)} %select_add_fusion.5), channel_id=1, source_target_pairs={{0,4},{4,8},{8,12},{1,5},{5,9},{9,13},{2,6},{6,10},{10,14},{3,7},{... | collective-permute-start | bytes 7077896 | tf_op jit(solution)/shard_map/ppermute | solution.py:135
  266.8 97.5 %collective-permute-start.11 = (f32[768,768]{1,0:T(8,128)S(1)}, f32[768,768]{1,0:T(8,128)S(1)}, u32[]{:S(2)}, u32[]{:S(2)}) collective-permute-start(f32[768,768]{1,0:T(8,128)S(1)} %select_add_fusion.4), channel_id=1, source_target_pairs={{4,0},{8,4},{12,8},{5,1},{9,5},{13,9},{6,2},{10,6},{14,10},{7,3},{... | collective-permute-start | bytes 7077896 | tf_op jit(solution)/shard_map/ppermute | solution.py:135
  274.0 107.7 %collective-permute-start.5 = (f32[768,768]{1,0:T(8,128)}, f32[768,768]{1,0:T(8,128)S(1)}, u32[]{:S(2)}, u32[]{:S(2)}) collective-permute-start(f32[768,768]{1,0:T(8,128)} %select_add_fusion.8), channel_id=1, source_target_pairs={{4,0},{8,4},{12,8},{5,1},{9,5},{13,9},{6,2},{10,6},{14,10},{7,3},{... | collective-permute-start | bytes 7077896 | tf_op jit(solution)/shard_map/ppermute | solution.py:135
  358.5 56.4 %collective-permute-start.14 = (f32[768,768]{1,0:T(8,128)}, f32[768,768]{1,0:T(8,128)}, u32[]{:S(2)}, u32[]{:S(2)}) collective-permute-start(f32[768,768]{1,0:T(8,128)} %select_add_fusion.1), channel_id=1, source_target_pairs={{0,4},{4,8},{8,12},{1,5},{5,9},{9,13},{2,6},{6,10},{10,14},{3,7},{... | collective-permute-start | bytes 7077896 | tf_op jit(solution)/shard_map/ppermute | solution.py:135
  369.4 56.4 %collective-permute-start.15 = (f32[768,768]{1,0:T(8,128)}, f32[768,768]{1,0:T(8,128)}, u32[]{:S(2)}, u32[]{:S(2)}) collective-permute-start(f32[768,768]{1,0:T(8,128)} %select_add_fusion), channel_id=1, source_target_pairs={{4,0},{8,4},{12,8},{5,1},{9,5},{13,9},{6,2},{10,6},{14,10},{7,3},{... | collective-permute-start | bytes 7077896 | tf_op jit(solution)/shard_map/ppermute | solution.py:135
  370.7 17.7 %slice-start.3 = ((s8[4718592]{0:T(1024)(128)(4,1)}), s8[4194304]{0:T(1024)(128)(4,1)S(1)}, s32[]{:S(2)}) async-start(s8[4718592]{0:T(1024)(128)(4,1)} %bitcast.107), calls=%async_computation.5 | async-start | bytes 8388608
  370.7 17.7 %slice-start.5 = ((s8[4718592]{0:T(1024)(128)(4,1)}), s8[4194304]{0:T(1024)(128)(4,1)S(1)}, s32[]{:S(2)}) async-start(s8[4718592]{0:T(1024)(128)(4,1)} %bitcast.114), calls=%async_computation.7 | async-start | bytes 8388608
  375.6 12.8 %slice-start.4 = ((s8[4718592]{0:T(1024)(128)(4,1)}), s8[524288]{0:T(1024)(128)(4,1)S(1)}, s32[]{:S(2)}) async-start(s8[4718592]{0:T(1024)(128)(4,1)} %bitcast.107), calls=%async_computation.6 | async-start | bytes 1048576
  375.7 12.8 %slice-start.6 = ((s8[4718592]{0:T(1024)(128)(4,1)}), s8[524288]{0:T(1024)(128)(4,1)S(1)}, s32[]{:S(2)}) async-start(s8[4718592]{0:T(1024)(128)(4,1)} %bitcast.114), calls=%async_computation.8 | async-start | bytes 1048576
  375.7 87.7 %collective-permute-start.12 = (f32[768,768]{1,0:T(8,128)}, f32[768,768]{1,0:T(8,128)}, u32[]{:S(2)}, u32[]{:S(2)}) collective-permute-start(f32[768,768]{1,0:T(8,128)} %select_add_fusion.3), channel_id=1, source_target_pairs={{0,4},{4,8},{8,12},{1,5},{5,9},{9,13},{2,6},{6,10},{10,14},{3,7},{... | collective-permute-start | bytes 7077896 | tf_op jit(solution)/shard_map/ppermute | solution.py:135
  386.9 87.0 %collective-permute-start.13 = (f32[768,768]{1,0:T(8,128)}, f32[768,768]{1,0:T(8,128)}, u32[]{:S(2)}, u32[]{:S(2)}) collective-permute-start(f32[768,768]{1,0:T(8,128)} %select_add_fusion.2), channel_id=1, source_target_pairs={{4,0},{8,4},{12,8},{5,1},{9,5},{13,9},{6,2},{10,6},{14,10},{7,3},{... | collective-permute-start | bytes 7077896 | tf_op jit(solution)/shard_map/ppermute | solution.py:135
  397.6 7.6 %copy-start.9 = (f32[768,768]{1,0:T(8,128)S(1)}, f32[768,768]{1,0:T(8,128)}, u32[]{:S(2)}) copy-start(f32[768,768]{1,0:T(8,128)} %fusion.68) | copy-start | bytes 7077892
  397.6 7.6 %copy-start.10 = (f32[768,768]{1,0:T(8,128)S(1)}, f32[768,768]{1,0:T(8,128)}, u32[]{:S(2)}) copy-start(f32[768,768]{1,0:T(8,128)} %fusion.84) | copy-start | bytes 7077892
  397.6 7.6 %copy-start.12 = (f32[768,768]{1,0:T(8,128)S(1)}, f32[768,768]{1,0:T(8,128)}, u32[]{:S(2)}) copy-start(f32[768,768]{1,0:T(8,128)} %fusion.85) | copy-start | bytes 7077892
  412.4 69.1 %copy-start.15 = (f32[768,768]{1,0:T(8,128)S(1)}, f32[768,768]{1,0:T(8,128)}, u32[]{:S(2)}) copy-start(f32[768,768]{1,0:T(8,128)} %add_negate_fusion.1) | copy-start | bytes 7077892
  412.4 69.1 %copy-start.16 = (f32[768,768]{1,0:T(8,128)S(1)}, f32[768,768]{1,0:T(8,128)}, u32[]{:S(2)}) copy-start(f32[768,768]{1,0:T(8,128)} %add_negate_fusion) | copy-start | bytes 7077892
  481.5 21.1 %copy-start.17 = (f32[1,3072]{1,0:T(1,128)S(1)}, f32[1,3072]{1,0:T(1,128)}, u32[]{:S(2)}) copy-start(f32[1,3072]{1,0:T(1,128)} %param.9) | copy-start | bytes 36868
  481.5 21.7 %copy-start.1 = (s32[1,4]{1,0:T(1,128)S(1)}, s32[1,4]{1,0:T(1,128)}, u32[]{:S(2)}) copy-start(s32[1,4]{1,0:T(1,128)} %param.7) | copy-start | bytes 52
  (11 other events, 44.5 us)
Sparse Core Ops, SparseCore 0:
  29.8 65.3 all-gather.4
  96.8 62.6 all-gather.6

commit v4 on v3

--- a/solution.py
+++ b/solution.py
@@ -107,6 +107,10 @@
             parent_inverse,
             *spread,
         )
+        if i == 1:
+            corner = sum(jnp.abs(x[0, 0]) for x in got[0])
+            corner = jnp.minimum(corner.astype(jnp.int32), 0)
+            local = jnp.where(corner >= 0, local, 0.0)
         pieces.append(lax.all_gather(local, "col", axis=0))
     blocks = jnp.concatenate(pieces, axis=0)
 

time: 520 us -> 512 us (0.985)
  waiting for transfers between devices: 205 us -> 199 us
    ppermute x4, waiting for transfers between devices: 69.4 us -> 63.4 us  [per_device(): lax.ppermute(spread[p], 'wide', perm)]
  transfers between devices with their start and end apart: 18 -> 18, of which waited for: 8 -> 10; matrix products, arithmetic and copies ran while one was open for 32% -> 33% of each run, Pallas kernels for 2% -> 2%
where the time goes in v4:
time: 512 us; the launch traced here: 504 us
  waiting for transfers between devices  199 us (39%)
  matrix products  157 us (31%)
  starting transfers between devices  55.1 us (11%)
  Pallas kernels  24.6 us (5%)
  other arithmetic  24 us (5%)
  between operations  16.3 us (3%)
  blocking collectives  15.6 us (3%)
  local copies, waits for them, and re-layouts  12.1 us (2%)
    dot_general x27, matrix products, dot(): lax.dot_general(a, b, ((contract[0], contract[1]), ((), ())), precision=l...  157 us
    ppermute x12, waiting for transfers between devices, per_device(): got[p][w] = flat(lax.ppermute(send, 'wide', perm))  136 us
    ppermute x4, waiting for transfers between devices, per_device(): lax.ppermute(spread[p], 'wide', perm)  63.4 us
    ppermute x12, starting transfers between devices, per_device(): got[p][w] = flat(lax.ppermute(send, 'wide', perm))  42.6 us
    pallas_call x2, Pallas kernels, per_device(): pl.pallas_call(pick_kernel, out_shape=jax.ShapeDtypeStruct((slots, slots)...  24.6 us
    psum x1, blocking collectives, per_device(): totals = lax.psum(partial_value, 'wide')  15.6 us
    ppermute x4, starting transfers between devices, per_device(): lax.ppermute(spread[p], 'wide', perm)  12.5 us
  transfers between devices with their start and end apart: 18, of which 10 were waited for; matrix products, arithmetic and copies ran while one was open for 33% of the time, Pallas kernels for 2%

profile of v4, /device:TPU:0, one launch (start us, length us, event | category | flops | bytes accessed | tf_op | source)
XLA Modules:
  0.0 504.1 jit_solution(2520085802024383890)
XLA Ops:
  14.5 12.3 %pick.2 = f32[768,768]{1,0:T(8,128)S(1)} custom-call(s32[1]{0:T(128)} %bitcast.at_ref, s32[768]{0:T(1024)S(1)} %get-tuple-element.15.mine_ref, f32[768,1]{1,0:T(8,128)S(1)} %fusion.61.live_ref, s32[1,768]{1,0:T(1,128)S(1)} %get-tuple-element.14.wanted_ref, f32[2048,4096]{1,0:T(8,128)} %parent_ref.3, f32[768,768]{1,0:T(8,128)S(1)} %get-tuple-element.9.rest_0_, ...), custom_call_target="tpu_custom_call" | custom-call | flops 1000 | bytes 1000 | tf_op jit(solution)/shard_map/pick/pallas_call | solution.py:87
  37.8 12.2 %pick.3 = f32[768,768]{1,0:T(8,128)S(1)} custom-call(s32[1]{0:T(128)} %bitcast.9.at_ref, s32[768]{0:T(1024)S(1)} %get-tuple-element.15.mine_ref, f32[768,1]{1,0:T(8,128)S(1)} %fusion.61.live_ref, s32[1,768]{1,0:T(1,128)S(1)} %get-tuple-element.13.wanted_ref, f32[2048,4096]{1,0:T(8,128)} %parent_ref.3, f32[768,768]{1,0:T(8,128)S(1)} %copy-done.3, ...), custom_call_target="tpu_custom_call" | custom-call | flops 1000 | bytes 1000 | tf_op jit(solution)/shard_map/pick/pallas_call | solution.py:87
  50.1 35.4 %collective-permute-done = f32[768,768]{1,0:T(8,128)S(1)} collective-permute-done((f32[768,768]{1,0:T(8,128)}, f32[768,768]{1,0:T(8,128)S(1)}, u32[]{:S(2)}, u32[]{:S(2)}) %collective-permute-start) | collective-permute-done | bytes 2359328 | tf_op jit(solution)/shard_map/ppermute | solution.py:77
  100.0 8.1 %select_add_fusion.11 = f32[768,768]{1,0:T(8,128)} fusion(f32[768,768]{1,0:T(8,128)} %copy-done.12, f32[768,3072]{1,0:T(8,128)} %bitcast.86, f32[2,768,768]{2,1,0:T(8,128)} %bitcast.103, s32[]{:T(128)S(6)} %select_n.317, pred[]{:T(512)S(6)} %le.24), kind=kOutput, calls=%fused_computation.62 | convolution fusion | flops 2719088640 | bytes 9437189 | tf_op jit(solution)/shard_map/dot_general | solution.py:46
  108.1 6.5 %collective-permute-start.2 = (f32[768,768]{1,0:T(8,128)}, f32[768,768]{1,0:T(8,128)}, u32[]{:S(2)}, u32[]{:S(2)}) collective-permute-start(f32[768,768]{1,0:T(8,128)} %select_add_fusion.11), channel_id=1, source_target_pairs={{0,4},{4,8},{8,12},{1,5},{5,9},{9,13},{2,6},{6,10},{10,14},{3,7},{... | collective-permute-start | bytes 7077896 | tf_op jit(solution)/shard_map/ppermute | solution.py:139
  114.6 8.0 %select_add_fusion.10 = f32[768,768]{1,0:T(8,128)} fusion(f32[768,768]{1,0:T(8,128)} %copy-done.10, f32[768,3072]{1,0:T(8,128)} %bitcast.87, f32[2,768,768]{2,1,0:T(8,128)} %bitcast.104, s32[]{:T(128)S(6)} %select_n.327, pred[]{:T(512)S(6)} %le.25), kind=kOutput, calls=%fused_computation.61 | convolution fusion | flops 2719088640 | bytes 9437189 | tf_op jit(solution)/shard_map/dot_general | solution.py:46
  123.8 25.0 %collective-permute-done.6 = f32[768,768]{1,0:T(8,128)} collective-permute-done((f32[768,768]{1,0:T(8,128)S(1)}, f32[768,768]{1,0:T(8,128)}, u32[]{:S(2)}, u32[]{:S(2)}) %collective-permute-start.6) | collective-permute-done | bytes 2359328 | tf_op jit(solution)/shard_map/ppermute | solution.py:77
  148.8 6.6 %select_add_fusion.7 = f32[768,768]{1,0:T(8,128)} fusion(f32[768,768]{1,0:T(8,128)} %collective-permute-done.6, f32[768,3072]{1,0:T(8,128)} %bitcast.88, f32[2,768,768]{2,1,0:T(8,128)S(1)} %bitcast.107, s32[]{:T(128)S(6)} %select_n.317, pred[]{:T(512)S(6)} %le.24), kind=kOutput, calls=%fused_computation.57 | convolution fusion | flops 2719088640 | bytes 9437189 | tf_op jit(solution)/shard_map/dot_general | solution.py:46
  155.5 5.9 %collective-permute-start.8 = (f32[768,768]{1,0:T(8,128)}, f32[768,768]{1,0:T(8,128)}, u32[]{:S(2)}, u32[]{:S(2)}) collective-permute-start(f32[768,768]{1,0:T(8,128)} %select_add_fusion.7), channel_id=1, source_target_pairs={{0,4},{4,8},{8,12},{1,5},{5,9},{9,13},{2,6},{6,10},{10,14},{3,7},{... | collective-permute-start | bytes 7077896 | tf_op jit(solution)/shard_map/ppermute | solution.py:139
  161.4 7.9 %select_add_fusion.6 = f32[768,768]{1,0:T(8,128)} fusion(f32[768,768]{1,0:T(8,128)} %collective-permute-done.7, f32[768,3072]{1,0:T(8,128)} %bitcast.89, f32[2,768,768]{2,1,0:T(8,128)} %bitcast.105, s32[]{:T(128)S(6)} %select_n.327, pred[]{:T(512)S(6)} %le.25), kind=kOutput, calls=%fused_computation.56 | convolution fusion | flops 2719088640 | bytes 9437189 | tf_op jit(solution)/shard_map/dot_general | solution.py:46
  171.1 6.8 %fusion.6 = (f32[768,768]{1,0:T(8,128)}, f32[768,768]{1,0:T(8,128)S(1)}, f32[768,768]{1,0:T(8,128)S(1)}, f32[768,768]{1,0:T(8,128)S(1)}, f32[768,768]{1,0:T(8,128)S(1)}) fusion(s32[]{:T(128)S(6)} %select_n.297, f32[2,768,768]{2,1,0:T(8,128)} %bitcast.106, f32[2,768,768]{2,1,0:T(8,128)} %bitcast.114, s32[]{:T(128)S(6)} %select_n.302, s32[]{:T(128)S(6)} %select_n.308, ...), kind=kLoop, calls=%fused_computation.24 | loop fusion | flops 2949120 | bytes 21233684 | tf_op jit(solution)/shard_map/jit(dynamic_index_in_dim)/squeeze | solution.py:121
  177.9 21.6 %collective-permute-done.2 = f32[768,768]{1,0:T(8,128)} collective-permute-done((f32[768,768]{1,0:T(8,128)}, f32[768,768]{1,0:T(8,128)}, u32[]{:S(2)}, u32[]{:S(2)}) %collective-permute-start.2) | collective-permute-done | bytes 2359328 | tf_op jit(solution)/shard_map/ppermute | solution.py:139
  209.3 5.9 %select_add_fusion.8 = f32[768,768]{1,0:T(8,128)} fusion(f32[768,768]{1,0:T(8,128)} %collective-permute-done.3, f32[768,768]{1,0:T(8,128)S(1)} %get-tuple-element.7, f32[768,3072]{1,0:T(8,128)S(1)} %bitcast.93, pred[]{:T(512)S(6)} %le.27), kind=kOutput, calls=%fused_computation.59 | convolution fusion | flops 2719088640 | bytes 9437185 | tf_op jit(solution)/shard_map/dot_general | solution.py:46
  216.6 33.5 %collective-permute-done.8 = f32[768,768]{1,0:T(8,128)} collective-permute-done((f32[768,768]{1,0:T(8,128)}, f32[768,768]{1,0:T(8,128)}, u32[]{:S(2)}, u32[]{:S(2)}) %collective-permute-start.8) | collective-permute-done | bytes 2359328 | tf_op jit(solution)/shard_map/ppermute | solution.py:139
  275.6 6.1 %fusion.82 = f32[768,768]{1,0:T(8,128)} fusion(f32[768,768]{1,0:T(8,128)S(1)} %get-tuple-element.7, f32[768,768]{1,0:T(8,128)} %collective-permute-done.2), kind=kOutput, calls=%fused_computation.104 | convolution fusion | flops 2717908992 | bytes 7077888 | tf_op jit(solution)/shard_map/dot_general | solution.py:46
  281.7 6.1 %fusion.83 = f32[768,768]{1,0:T(8,128)} fusion(f32[768,768]{1,0:T(8,128)S(1)} %get-tuple-element.8, f32[768,768]{1,0:T(8,128)} %collective-permute-done.3), kind=kOutput, calls=%fused_computation.105 | convolution fusion | flops 2717908992 | bytes 7077888 | tf_op jit(solution)/shard_map/dot_general | solution.py:46
  287.8 6.1 %fusion.87 = f32[768,768]{1,0:T(8,128)} fusion(f32[768,768]{1,0:T(8,128)S(1)} %get-tuple-element.8, f32[768,768]{1,0:T(8,128)} %collective-permute-done.9), kind=kOutput, calls=%fused_computation.109 | convolution fusion | flops 2717908992 | bytes 7077888 | tf_op jit(solution)/shard_map/dot_general | solution.py:46
  293.9 5.3 %fusion.86 = f32[768,768]{1,0:T(8,128)S(1)} fusion(f32[768,768]{1,0:T(8,128)S(1)} %get-tuple-element.7, f32[768,768]{1,0:T(8,128)} %collective-permute-done.8), kind=kOutput, calls=%fused_computation.108 | convolution fusion | flops 2717908992 | bytes 7077888 | tf_op jit(solution)/shard_map/dot_general | solution.py:46
  303.9 6.3 %fusion.84 = f32[768,768]{1,0:T(8,128)} fusion(f32[768,768]{1,0:T(8,128)S(1)} %get-tuple-element.5, f32[768,768]{1,0:T(8,128)} %collective-permute-done.6), kind=kOutput, calls=%fused_computation.106 | convolution fusion | flops 2717908992 | bytes 7077888 | tf_op jit(solution)/shard_map/dot_general | solution.py:46
  314.7 6.3 %fusion.85 = f32[768,768]{1,0:T(8,128)} fusion(f32[768,768]{1,0:T(8,128)S(1)} %get-tuple-element.6, f32[768,768]{1,0:T(8,128)} %collective-permute-done.7), kind=kOutput, calls=%fused_computation.107 | convolution fusion | flops 2717908992 | bytes 7077888 | tf_op jit(solution)/shard_map/dot_general | solution.py:46
  321.0 7.5 %fusion.1 = f32[768,1536]{1,0:T(8,128)} fusion(f32[768,768]{1,0:T(8,128)S(1)} %copy-done.6, f32[768,3072]{1,0:T(8,128)S(1)} %bitcast.98), kind=kOutput, calls=%fused_computation.19 | convolution fusion | flops 5435817984 | bytes 11796480 | tf_op jit(solution)/shard_map/dot_general | solution.py:46
  328.5 20.3 %collective-permute-done.10 = f32[768,768]{1,0:T(8,128)S(1)} collective-permute-done((f32[768,768]{1,0:T(8,128)S(1)}, f32[768,768]{1,0:T(8,128)S(1)}, u32[]{:S(2)}, u32[]{:S(2)}) %collective-permute-start.10) | collective-permute-done | bytes 2359328 | tf_op jit(solution)/shard_map/ppermute | solution.py:139
  353.7 5.8 %collective-permute-start.14 = (f32[768,768]{1,0:T(8,128)}, f32[768,768]{1,0:T(8,128)}, u32[]{:S(2)}, u32[]{:S(2)}) collective-permute-start(f32[768,768]{1,0:T(8,128)} %select_add_fusion.1), channel_id=1, source_target_pairs={{0,4},{4,8},{8,12},{1,5},{5,9},{9,13},{2,6},{6,10},{10,14},{3,7},{... | collective-permute-start | bytes 7077896 | tf_op jit(solution)/shard_map/ppermute | solution.py:139
  370.8 6.1 %collective-permute-start.12 = (f32[768,768]{1,0:T(8,128)}, f32[768,768]{1,0:T(8,128)}, u32[]{:S(2)}, u32[]{:S(2)}) collective-permute-start(f32[768,768]{1,0:T(8,128)} %select_add_fusion.3), channel_id=1, source_target_pairs={{0,4},{4,8},{8,12},{1,5},{5,9},{9,13},{2,6},{6,10},{10,14},{3,7},{... | collective-permute-start | bytes 7077896 | tf_op jit(solution)/shard_map/ppermute | solution.py:139
  392.6 7.6 %add_negate_fusion.1 = f32[768,768]{1,0:T(8,128)} fusion(f32[768,768]{1,0:T(8,128)} %fusion.74, f32[768,768]{1,0:T(8,128)} %fusion.83, f32[768,768]{1,0:T(8,128)} %fusion.82, f32[768,768]{1,0:T(8,128)} %fusion.81, f32[768,768]{1,0:T(8,128)S(1)} %copy-done.9, f32[768,768]{1,0:T(8,128)} %fusion.80, f32[768,768]{1,0:T(8,128)} %copy-done.14, pred[]{:T(512)S(6)} %ge.33, ...), kind=kOutput, calls=%fused_computation.58 | convolution fusion | flops 2726166528 | bytes 28311562 | tf_op jit(solution)/shard_map/dot_general | solution.py:46
  400.2 7.1 %add_negate_fusion = f32[768,768]{1,0:T(8,128)} fusion(f32[768,768]{1,0:T(8,128)} %fusion.72, f32[768,768]{1,0:T(8,128)S(1)} %copy-done.8, f32[768,768]{1,0:T(8,128)S(1)} %fusion.86, f32[768,768]{1,0:T(8,128)} %fusion.85, f32[768,768]{1,0:T(8,128)S(1)} %copy-done.7, f32[768,768]{1,0:T(8,128)} %fusion.84, f32[768,768]{1,0:T(8,128)} %copy-done.15, ...), kind=kOutput, calls=%fused_computation.53 | convolution fusion | flops 2726166528 | bytes 28311562 | tf_op jit(solution)/shard_map/dot_general | solution.py:46
  410.1 10.6 %collective-permute-done.15 = f32[768,768]{1,0:T(8,128)} collective-permute-done((f32[768,768]{1,0:T(8,128)}, f32[768,768]{1,0:T(8,128)}, u32[]{:S(2)}, u32[]{:S(2)}) %collective-permute-start.15) | collective-permute-done | bytes 2359328 | tf_op jit(solution)/shard_map/ppermute | solution.py:139
  420.7 36.8 %collective-permute-done.12 = f32[768,768]{1,0:T(8,128)} collective-permute-done((f32[768,768]{1,0:T(8,128)}, f32[768,768]{1,0:T(8,128)}, u32[]{:S(2)}, u32[]{:S(2)}) %collective-permute-start.12) | collective-permute-done | bytes 2359328 | tf_op jit(solution)/shard_map/ppermute | solution.py:139
  457.5 10.3 %collective-permute-done.13 = f32[768,768]{1,0:T(8,128)} collective-permute-done((f32[768,768]{1,0:T(8,128)}, f32[768,768]{1,0:T(8,128)}, u32[]{:S(2)}, u32[]{:S(2)}) %collective-permute-start.13) | collective-permute-done | bytes 2359328 | tf_op jit(solution)/shard_map/ppermute | solution.py:139
  467.8 7.4 %fusion.20 = (f32[768,768]{1,0:T(8,128)S(1)}, f32[768,768]{1,0:T(8,128)}) fusion(f32[768,768]{1,0:T(8,128)} %collective-permute-done.13, f32[768,768]{1,0:T(8,128)} %collective-permute-done.12, f32[768,1536]{1,0:T(8,128)} %fusion.1, f32[768,768]{1,0:T(8,128)} %collective-permute-done.15, f32[768,768]{1,0:T(8,128)} %collective-permute-done.14), kind=kLoop, calls=%fused_computation.40 | loop fusion | flops 3538944 | bytes 18874368 | tf_op jit(solution)/shard_map/neg | solution.py:143
  475.2 5.5 %multiply_reduce_fusion = (f32[3072]{0:T(1024)S(1)}, f32[1,768,3072]{2,1,0:T(8,128)}) fusion(f32[768,768]{1,0:T(8,128)} %get-tuple-element.12, f32[768,768]{1,0:T(8,128)S(1)} %get-tuple-element.11, f32[768,768]{1,0:T(8,128)S(1)} %copy-done.17, f32[768,768]{1,0:T(8,128)S(1)} %copy-done.16, f32[1,768,3072]{2,1,0:T(8,128)S(1)} %bitcast.91), kind=kLoop, calls=%fused_computation.17 | loop fusion | flops 11793408 | bytes 28323840 | tf_op jit(solution)/shard_map/reduce_sum | solution.py:145
  480.7 15.6 %psum.7 = f32[3072]{0:T(1024)S(1)} all-reduce(f32[3072]{0:T(1024)S(1)} %get-tuple-element.2), channel_id=1, replica_groups=mesh['parts'=2,'wide'=4,'col'=2,'sub'=2] {'wide'}, use_global_device_ids=true, to_apply=%region_1.2 | all-reduce | flops 3072 | bytes 24576 | tf_op jit(solution)/shard_map/psum | solution.py:146
  (114 shorter events, 115.3 us)
Async XLA Ops:
  7.2 92.8 %all-gather.5.cloned.1.call-start = ((), (), s32[]{:S(2)}) async-start(), calls=%async_computation | async-start | bytes 7077888 | tf_op jit(solution)/shard_map/all_gather | solution.py:114
  29.7 141.4 %all-gather.7.cloned.1.call-start = ((), (), s32[]{:S(2)}) async-start(), calls=%async_computation.1 | async-start | bytes 7077888 | tf_op jit(solution)/shard_map/all_gather | solution.py:114
  29.8 55.7 %collective-permute-start = (f32[768,768]{1,0:T(8,128)}, f32[768,768]{1,0:T(8,128)S(1)}, u32[]{:S(2)}, u32[]{:S(2)}) collective-permute-start(f32[768,768]{1,0:T(8,128)} %copy-done.2), channel_id=1, source_target_pairs={{0,4},{4,8},{8,12},{1,5},{5,9},{9,13},{2,6},{6,10},{10,14},{3,7},{... | collective-permute-start | bytes 7077896 | tf_op jit(solution)/shard_map/ppermute | solution.py:77
  34.9 54.8 %collective-permute-start.1 = (f32[768,768]{1,0:T(8,128)}, f32[768,768]{1,0:T(8,128)S(1)}, u32[]{:S(2)}, u32[]{:S(2)}) collective-permute-start(f32[768,768]{1,0:T(8,128)} %copy-done.2), channel_id=1, source_target_pairs={{4,0},{8,4},{12,8},{5,1},{9,5},{13,9},{6,2},{10,6},{14,10},{7,3},{... | collective-permute-start | bytes 7077896 | tf_op jit(solution)/shard_map/ppermute | solution.py:77
  93.8 55.0 %collective-permute-start.6 = (f32[768,768]{1,0:T(8,128)S(1)}, f32[768,768]{1,0:T(8,128)}, u32[]{:S(2)}, u32[]{:S(2)}) collective-permute-start(f32[768,768]{1,0:T(8,128)S(1)} %get-tuple-element.10.rest_1_), channel_id=1, source_target_pairs={{0,4},{4,8},{8,12},{1,5},{5,9},{9,13},{2,6},{6,10},{10,14},{3,7},{... | collective-permute-start | bytes 7077896 | tf_op jit(solution)/shard_map/ppermute | solution.py:77
  98.6 62.8 %collective-permute-start.7 = (f32[768,768]{1,0:T(8,128)S(1)}, f32[768,768]{1,0:T(8,128)}, u32[]{:S(2)}, u32[]{:S(2)}) collective-permute-start(f32[768,768]{1,0:T(8,128)S(1)} %get-tuple-element.10.rest_1_), channel_id=1, source_target_pairs={{4,0},{8,4},{12,8},{5,1},{9,5},{13,9},{6,2},{10,6},{14,10},{7,3},{... | collective-permute-start | bytes 7077896 | tf_op jit(solution)/shard_map/ppermute | solution.py:77
  108.1 91.4 %collective-permute-start.2 = (f32[768,768]{1,0:T(8,128)}, f32[768,768]{1,0:T(8,128)}, u32[]{:S(2)}, u32[]{:S(2)}) collective-permute-start(f32[768,768]{1,0:T(8,128)} %select_add_fusion.11), channel_id=1, source_target_pairs={{0,4},{4,8},{8,12},{1,5},{5,9},{9,13},{2,6},{6,10},{10,14},{3,7},{... | collective-permute-start | bytes 7077896 | tf_op jit(solution)/shard_map/ppermute | solution.py:139
  114.6 34.3 %copy-start.5 = (f32[1536,768]{1,0:T(8,128)S(1)}, f32[1536,768]{1,0:T(8,128)}, u32[]{:S(2)}) copy-start(f32[1536,768]{1,0:T(8,128)} %all-gather.5.cloned.1.call-done) | copy-start | bytes 14155780
  122.5 86.7 %collective-permute-start.3 = (f32[768,768]{1,0:T(8,128)}, f32[768,768]{1,0:T(8,128)}, u32[]{:S(2)}, u32[]{:S(2)}) collective-permute-start(f32[768,768]{1,0:T(8,128)} %select_add_fusion.10), channel_id=1, source_target_pairs={{4,0},{8,4},{12,8},{5,1},{9,5},{13,9},{6,2},{10,6},{14,10},{7,3},{... | collective-permute-start | bytes 7077896 | tf_op jit(solution)/shard_map/ppermute | solution.py:139
  155.5 94.6 %collective-permute-start.8 = (f32[768,768]{1,0:T(8,128)}, f32[768,768]{1,0:T(8,128)}, u32[]{:S(2)}, u32[]{:S(2)}) collective-permute-start(f32[768,768]{1,0:T(8,128)} %select_add_fusion.7), channel_id=1, source_target_pairs={{0,4},{4,8},{8,12},{1,5},{5,9},{9,13},{2,6},{6,10},{10,14},{3,7},{... | collective-permute-start | bytes 7077896 | tf_op jit(solution)/shard_map/ppermute | solution.py:139
  161.4 38.1 %slice-start = ((s8[9437184]{0:T(1024)(128)(4,1)}), s8[1048576]{0:T(1024)(128)(4,1)S(1)}, s32[]{:S(2)}) async-start(s8[9437184]{0:T(1024)(128)(4,1)} %bitcast.90), calls=%async_computation.2 | async-start | bytes 2097152
  169.4 99.5 %collective-permute-start.9 = (f32[768,768]{1,0:T(8,128)}, f32[768,768]{1,0:T(8,128)}, u32[]{:S(2)}, u32[]{:S(2)}) collective-permute-start(f32[768,768]{1,0:T(8,128)} %select_add_fusion.6), channel_id=1, source_target_pairs={{4,0},{8,4},{12,8},{5,1},{9,5},{13,9},{6,2},{10,6},{14,10},{7,3},{... | collective-permute-start | bytes 7077896 | tf_op jit(solution)/shard_map/ppermute | solution.py:139
  171.1 28.4 %slice-start.1 = ((s8[9437184]{0:T(1024)(128)(4,1)}), s8[4194304]{0:T(1024)(128)(4,1)S(1)}, s32[]{:S(2)}) async-start(s8[9437184]{0:T(1024)(128)(4,1)} %bitcast.90), calls=%async_computation.3 | async-start | bytes 8388608
  171.1 28.4 %slice-start.2 = ((s8[9437184]{0:T(1024)(128)(4,1)}), s8[4194304]{0:T(1024)(128)(4,1)S(1)}, s32[]{:S(2)}) async-start(s8[9437184]{0:T(1024)(128)(4,1)} %bitcast.90), calls=%async_computation.4 | async-start | bytes 8388608
  204.7 161.1 %collective-permute-start.4 = (f32[768,768]{1,0:T(8,128)S(1)}, f32[768,768]{1,0:T(8,128)S(1)}, u32[]{:S(2)}, u32[]{:S(2)}) collective-permute-start(f32[768,768]{1,0:T(8,128)S(1)} %select_add_fusion.9), channel_id=1, source_target_pairs={{0,4},{4,8},{8,12},{1,5},{5,9},{9,13},{2,6},{6,10},{10,14},{3,7},{... | collective-permute-start | bytes 7077896 | tf_op jit(solution)/shard_map/ppermute | solution.py:139
  215.2 44.8 %copy-start.6 = (f32[768,768]{1,0:T(8,128)S(1)}, f32[768,768]{1,0:T(8,128)}, u32[]{:S(2)}) copy-start(f32[768,768]{1,0:T(8,128)} %get-tuple-element.4) | copy-start | bytes 7077892
  215.2 161.8 %collective-permute-start.5 = (f32[768,768]{1,0:T(8,128)}, f32[768,768]{1,0:T(8,128)S(1)}, u32[]{:S(2)}, u32[]{:S(2)}) collective-permute-start(f32[768,768]{1,0:T(8,128)} %select_add_fusion.8), channel_id=1, source_target_pairs={{4,0},{8,4},{12,8},{5,1},{9,5},{13,9},{6,2},{10,6},{14,10},{7,3},{... | collective-permute-start | bytes 7077896 | tf_op jit(solution)/shard_map/ppermute | solution.py:139
  255.2 93.6 %collective-permute-start.10 = (f32[768,768]{1,0:T(8,128)S(1)}, f32[768,768]{1,0:T(8,128)S(1)}, u32[]{:S(2)}, u32[]{:S(2)}) collective-permute-start(f32[768,768]{1,0:T(8,128)S(1)} %select_add_fusion.5), channel_id=1, source_target_pairs={{0,4},{4,8},{8,12},{1,5},{5,9},{9,13},{2,6},{6,10},{10,14},{3,7},{... | collective-permute-start | bytes 7077896 | tf_op jit(solution)/shard_map/ppermute | solution.py:139
  274.1 85.4 %collective-permute-start.11 = (f32[768,768]{1,0:T(8,128)S(1)}, f32[768,768]{1,0:T(8,128)S(1)}, u32[]{:S(2)}, u32[]{:S(2)}) collective-permute-start(f32[768,768]{1,0:T(8,128)S(1)} %select_add_fusion.4), channel_id=1, source_target_pairs={{4,0},{8,4},{12,8},{5,1},{9,5},{13,9},{6,2},{10,6},{14,10},{7,3},{... | collective-permute-start | bytes 7077896 | tf_op jit(solution)/shard_map/ppermute | solution.py:139
  353.7 56.4 %collective-permute-start.14 = (f32[768,768]{1,0:T(8,128)}, f32[768,768]{1,0:T(8,128)}, u32[]{:S(2)}, u32[]{:S(2)}) collective-permute-start(f32[768,768]{1,0:T(8,128)} %select_add_fusion.1), channel_id=1, source_target_pairs={{0,4},{4,8},{8,12},{1,5},{5,9},{9,13},{2,6},{6,10},{10,14},{3,7},{... | collective-permute-start | bytes 7077896 | tf_op jit(solution)/shard_map/ppermute | solution.py:139
  364.3 56.4 %collective-permute-start.15 = (f32[768,768]{1,0:T(8,128)}, f32[768,768]{1,0:T(8,128)}, u32[]{:S(2)}, u32[]{:S(2)}) collective-permute-start(f32[768,768]{1,0:T(8,128)} %select_add_fusion), channel_id=1, source_target_pairs={{4,0},{8,4},{12,8},{5,1},{9,5},{13,9},{6,2},{10,6},{14,10},{7,3},{... | collective-permute-start | bytes 7077896 | tf_op jit(solution)/shard_map/ppermute | solution.py:139
  365.8 17.6 %slice-start.3 = ((s8[4718592]{0:T(1024)(128)(4,1)}), s8[4194304]{0:T(1024)(128)(4,1)S(1)}, s32[]{:S(2)}) async-start(s8[4718592]{0:T(1024)(128)(4,1)} %bitcast.108), calls=%async_computation.5 | async-start | bytes 8388608
  365.8 17.6 %slice-start.5 = ((s8[4718592]{0:T(1024)(128)(4,1)}), s8[4194304]{0:T(1024)(128)(4,1)S(1)}, s32[]{:S(2)}) async-start(s8[4718592]{0:T(1024)(128)(4,1)} %bitcast.115), calls=%async_computation.7 | async-start | bytes 8388608
  370.8 12.6 %slice-start.4 = ((s8[4718592]{0:T(1024)(128)(4,1)}), s8[524288]{0:T(1024)(128)(4,1)S(1)}, s32[]{:S(2)}) async-start(s8[4718592]{0:T(1024)(128)(4,1)} %bitcast.108), calls=%async_computation.6 | async-start | bytes 1048576
  370.8 12.6 %slice-start.6 = ((s8[4718592]{0:T(1024)(128)(4,1)}), s8[524288]{0:T(1024)(128)(4,1)S(1)}, s32[]{:S(2)}) async-start(s8[4718592]{0:T(1024)(128)(4,1)} %bitcast.115), calls=%async_computation.8 | async-start | bytes 1048576
  370.8 86.7 %collective-permute-start.12 = (f32[768,768]{1,0:T(8,128)}, f32[768,768]{1,0:T(8,128)}, u32[]{:S(2)}, u32[]{:S(2)}) collective-permute-start(f32[768,768]{1,0:T(8,128)} %select_add_fusion.3), channel_id=1, source_target_pairs={{0,4},{4,8},{8,12},{1,5},{5,9},{9,13},{2,6},{6,10},{10,14},{3,7},{... | collective-permute-start | bytes 7077896 | tf_op jit(solution)/shard_map/ppermute | solution.py:139
  381.7 86.0 %collective-permute-start.13 = (f32[768,768]{1,0:T(8,128)}, f32[768,768]{1,0:T(8,128)}, u32[]{:S(2)}, u32[]{:S(2)}) collective-permute-start(f32[768,768]{1,0:T(8,128)} %select_add_fusion.2), channel_id=1, source_target_pairs={{4,0},{8,4},{12,8},{5,1},{9,5},{13,9},{6,2},{10,6},{14,10},{7,3},{... | collective-permute-start | bytes 7077896 | tf_op jit(solution)/shard_map/ppermute | solution.py:139
  392.6 7.6 %copy-start.8 = (f32[768,768]{1,0:T(8,128)S(1)}, f32[768,768]{1,0:T(8,128)}, u32[]{:S(2)}) copy-start(f32[768,768]{1,0:T(8,128)} %fusion.87) | copy-start | bytes 7077892
  407.3 67.8 %copy-start.16 = (f32[768,768]{1,0:T(8,128)S(1)}, f32[768,768]{1,0:T(8,128)}, u32[]{:S(2)}) copy-start(f32[768,768]{1,0:T(8,128)} %add_negate_fusion.1) | copy-start | bytes 7077892
  407.3 67.8 %copy-start.17 = (f32[768,768]{1,0:T(8,128)S(1)}, f32[768,768]{1,0:T(8,128)}, u32[]{:S(2)}) copy-start(f32[768,768]{1,0:T(8,128)} %add_negate_fusion) | copy-start | bytes 7077892
  475.2 21.1 %copy-start.20 = (f32[1,3072]{1,0:T(1,128)S(1)}, f32[1,3072]{1,0:T(1,128)}, u32[]{:S(2)}) copy-start(f32[1,3072]{1,0:T(1,128)} %param.9) | copy-start | bytes 36868
  475.2 21.7 %copy-start.1 = (s32[1,4]{1,0:T(1,128)S(1)}, s32[1,4]{1,0:T(1,128)}, u32[]{:S(2)}) copy-start(s32[1,4]{1,0:T(1,128)} %param.7) | copy-start | bytes 52
  (14 other events, 59.2 us)
Sparse Core Ops, SparseCore 0:
  29.8 65.3 all-gather.4
  96.8 62.6 all-gather.6
